TPU v7x, 256 devices: a whole 4x4x8 slice. The times are simulated.
256 devices in a mesh: dp: 2 (over core), row: 8 (over y, x_hi), col: 16 (over x_lo, z).
Axes of the slice: x: 4 (x_hi: 2, x_lo: 2; x = x_hi * 2 + x_lo), y: 4, z: 8, core: 2. Of those that a mesh axis runs over, the one named last changes fastest.
Arguments:
- tokens: bfloat16 [4096, 4096], P(('dp', 'col'), 'row'), may hold values from -6 to 6
- cotangent: bfloat16 [4096, 4096], P(('dp', 'col'), 'row'), may hold values from -6 to 6
- gate_blocks: bfloat16 [128, 4, 128, 128], P(('row', 'col')), may hold values from -0.3125 to 0.3125
- up_blocks: bfloat16 [128, 4, 128, 128], P(('row', 'col')), may hold values from -0.3125 to 0.3125
- down_blocks: bfloat16 [128, 4, 128, 128], P(('row', 'col')), may hold values from -0.15625 to 0.15625
- gate_index: int32 [128, 4], replicated, may hold values from 0 to 32, as said below
- up_index: int32 [128, 4], replicated, may hold values from 0 to 32, as said below
- down_index: int32 [128, 4], replicated, may hold values from 0 to 32, as said below
Outputs:
- block_output: bfloat16 [4096, 4096], P(('dp', 'col'), 'row')
- input_grad: bfloat16 [4096, 4096], P(('dp', 'col'), 'row')
- gate_grad: float32 [128, 4, 128, 128], P(('row', 'col'))
- up_grad: float32 [128, 4, 128, 128], P(('row', 'col'))
- down_grad: float32 [128, 4, 128, 128], P(('row', 'col'))
Inputs may be any that keep to these rules, and one draw needn't show every extreme that they name: `gate_index`: in each panel's row the used slots come first and hold distinct block numbers in ascending order; the other slots hold 32. Each panel uses 2 to 4 slots, and some panel uses all 4. `up_index`: as for gate_index. `down_index`: as for gate_index.
All inputs are finite; a program needn't handle non-finite values.
Results may differ from a plain program's by a relative error of at most 0.023.
Values may be sent and summed in bfloat16 or wider, within the bound.
A program may use at most 128 MiB of HBM per device.

v0:
```python
import jax
import jax.numpy as jnp
from jax import lax
from jax.sharding import PartitionSpec as P

D = 4096
BLK = 128


def pick_blocks(blocks, slot_index, block_count):
    return jnp.take(blocks, jnp.minimum(slot_index, block_count - 1), axis=1)


def per_device(
    tokens, cotangent, gate_blocks, up_blocks, down_blocks, gate_index, up_index, down_index
):
    block_count = D // BLK
    full_tokens, full_cotangent = (
        lax.all_gather(tokens, "row", axis=1, tiled=True),
        lax.all_gather(cotangent, "row", axis=1, tiled=True),
    )
    row_count = full_tokens.shape[0]
    token_blocks = full_tokens.reshape(row_count, block_count, BLK)
    cotan_blocks = full_cotangent.reshape(row_count, block_count, BLK)
    owned_panels = gate_blocks.shape[0]
    group_panels = lax.axis_size("col") * owned_panels
    group_start = lax.axis_index("row") * group_panels
    group_gate = lax.dynamic_slice_in_dim(gate_index, group_start, group_panels, 0)
    group_up = lax.dynamic_slice_in_dim(up_index, group_start, group_panels, 0)
    group_down = lax.dynamic_slice_in_dim(down_index, group_start, group_panels, 0)
    zero_acc = jnp.zeros((row_count, block_count, BLK), jnp.float32)
    out_acc = zero_acc
    in_acc = zero_acc
    w_gate = lax.all_gather(gate_blocks, "col", axis=0, tiled=True)
    w_up = lax.all_gather(up_blocks, "col", axis=0, tiled=True)
    w_down = lax.all_gather(down_blocks, "col", axis=0, tiled=True)
    slot_gate = group_gate
    slot_up = group_up
    slot_down = group_down
    w_gate = w_gate * (slot_gate < block_count).astype(jnp.bfloat16)[:, :, None, None]
    w_up = w_up * (slot_up < block_count).astype(jnp.bfloat16)[:, :, None, None]
    w_down = w_down * (slot_down < block_count).astype(jnp.bfloat16)[:, :, None, None]
    x_gate = pick_blocks(token_blocks, slot_gate, block_count)
    x_up = pick_blocks(token_blocks, slot_up, block_count)
    dy_down = pick_blocks(cotan_blocks, slot_down, block_count)
    gate = jnp.einsum("tnsb,nsbo->tno", x_gate, w_gate, preferred_element_type=jnp.float32)
    up_value = jnp.einsum("tnsb,nsbo->tno", x_up, w_up, preferred_element_type=jnp.float32)
    sigmoid_gate = jax.nn.sigmoid(gate)
    swish_gate = gate * sigmoid_gate
    activated = (swish_gate * up_value).astype(jnp.bfloat16)
    spread_down = jnp.einsum(
        "tni,nsio->tnso", activated, w_down, preferred_element_type=jnp.float32
    )
    down_target = jnp.minimum(slot_down, block_count - 1).reshape(-1)
    out_acc = out_acc.at[:, down_target].add(spread_down.reshape(row_count, -1, BLK))
    act_grad = jnp.einsum("tnso,nsio->tni", dy_down, w_down, preferred_element_type=jnp.float32)
    silu_slope = sigmoid_gate * (1.0 + gate * (1.0 - sigmoid_gate))
    gate_delta = (act_grad * up_value * silu_slope).astype(jnp.bfloat16)
    up_delta = (act_grad * swish_gate).astype(jnp.bfloat16)
    back_gate = jnp.einsum("tno,nsbo->tnsb", gate_delta, w_gate, preferred_element_type=jnp.float32)
    back_up = jnp.einsum("tno,nsbo->tnsb", up_delta, w_up, preferred_element_type=jnp.float32)
    in_target = jnp.concatenate(
        (
            jnp.minimum(slot_gate, block_count - 1).reshape(-1),
            jnp.minimum(slot_up, block_count - 1).reshape(-1),
        ),
        axis=0,
    )
    in_terms = jnp.concatenate(
        (back_gate.reshape(row_count, -1, BLK), back_up.reshape(row_count, -1, BLK)), axis=1
    )
    in_acc = in_acc.at[:, in_target].add(in_terms)
    out_acc, in_acc, act_all, gate_all, up_all = (out_acc, in_acc, activated, gate_delta, up_delta)
    out_share, in_share = (
        lax.psum_scatter(
            out_acc.astype(jnp.bfloat16), "row", scatter_dimension=1, tiled=True
        ).astype(jnp.float32),
        lax.psum_scatter(
            in_acc.astype(jnp.bfloat16), "row", scatter_dimension=1, tiled=True
        ).astype(jnp.float32),
    )
    block_output = out_share.reshape(row_count, -1).astype(jnp.bfloat16)
    input_grad = in_share.reshape(row_count, -1).astype(jnp.bfloat16)
    slot_gate = group_gate
    slot_up = group_up
    slot_down = group_down
    x_gate = pick_blocks(token_blocks, slot_gate, block_count)
    x_up = pick_blocks(token_blocks, slot_up, block_count)
    dy_down = pick_blocks(cotan_blocks, slot_down, block_count)
    gate_part = jnp.einsum("tnsb,tno->nsbo", x_gate, gate_all, preferred_element_type=jnp.float32)
    up_part = jnp.einsum("tnsb,tno->nsbo", x_up, up_all, preferred_element_type=jnp.float32)
    down_part = jnp.einsum("tni,tnso->nsio", act_all, dy_down, preferred_element_type=jnp.float32)
    gate_part = gate_part * (slot_gate < block_count).astype(jnp.float32)[:, :, None, None]
    up_part = up_part * (slot_up < block_count).astype(jnp.float32)[:, :, None, None]
    down_part = down_part * (slot_down < block_count).astype(jnp.float32)[:, :, None, None]
    owned_sum = lax.psum_scatter(
        jnp.stack((gate_part, up_part, down_part), axis=1).astype(jnp.bfloat16),
        "col",
        scatter_dimension=0,
        tiled=True,
    )
    grad_total = lax.psum(owned_sum, "dp").astype(jnp.float32)
    return (block_output, input_grad, grad_total[:, 0], grad_total[:, 1], grad_total[:, 2])


def solution(mesh):
    return jax.shard_map(
        per_device,
        mesh=mesh,
        in_specs=(
            P(("dp", "col"), "row"),
            P(("dp", "col"), "row"),
            P(("row", "col"), None, None, None),
            P(("row", "col"), None, None, None),
            P(("row", "col"), None, None, None),
            P(),
            P(),
            P(),
        ),
        out_specs=(
            P(("dp", "col"), "row"),
            P(("dp", "col"), "row"),
            P(("row", "col"), None, None, None),
            P(("row", "col"), None, None, None),
            P(("row", "col"), None, None, None),
        ),
        check_vma=False,
    )
```

profile of v0, /device:TPU:1, one launch (start us, length us, event | category | flops | bytes accessed | tf_op | source)
XLA Modules:
  0.0 706.0 jit_solution(9957376051797089912)
XLA Ops:
  7.2 1.7 copy.132
  8.9 1.7 copy.152
  15.6 49.4 %all-gather.10.cloned.1.call-done = bf16[128,4096]{0,1:T(8,128)(2,1)} async-done(((bf16[128,512]{0,1:T(8,128)(2,1)}), bf16[128,4096]{0,1:T(8,128)(2,1)}) %all-gather.10.cloned.1.call-update) | async-done | bytes 1048592 | tf_op jit(solution)/shard_map/all_gather | solution.py:19
  65.0 1.6 copy.134
  66.6 51.9 %all-gather.14.cloned.1.call-done = bf16[128,4096]{0,1:T(8,128)(2,1)} async-done(((bf16[128,512]{0,1:T(8,128)(2,1)}), bf16[128,4096]{0,1:T(8,128)(2,1)}) %all-gather.14.cloned.1.call-update) | async-done | bytes 1048592 | tf_op jit(solution)/shard_map/all_gather | solution.py:20
  118.5 1.6 copy.154
  120.1 2.2 gather_fusion.2
  122.3 3.9 copy.155
  127.2 2.6 copy.142
  130.7 2.6 copy.135
  133.4 49.1 %all-gather.8.cloned.1.call-done = bf16[16,4,128,128]{3,2,1,0:T(8,128)(2,1)} async-done(((bf16[1,4,128,128]{3,2,1,0:T(8,128)(2,1)}), bf16[16,4,128,128]{3,2,1,0:T(8,128)(2,1)}) %all-gather.8.cloned.1.call-update) | async-done | bytes 2097168 | tf_op jit(solution)/shard_map/all_gather | solution.py:34
  182.5 4.2 fusion.27
  186.6 66.3 %all-gather.12.cloned.1.call-done = bf16[16,4,128,128]{3,2,1,0:T(8,128)(2,1)} async-done(((bf16[1,4,128,128]{3,2,1,0:T(8,128)(2,1)}), bf16[16,4,128,128]{3,2,1,0:T(8,128)(2,1)}) %all-gather.12.cloned.1.call-update) | async-done | bytes 2097168 | tf_op jit(solution)/shard_map/all_gather | solution.py:35
  252.9 4.2 fusion.32
  257.1 66.2 %all-gather.6.cloned.1.call-done = bf16[16,4,128,128]{3,2,1,0:T(8,128)(2,1)} async-done(((bf16[1,4,128,128]{3,2,1,0:T(8,128)(2,1)}), bf16[16,4,128,128]{3,2,1,0:T(8,128)(2,1)}) %all-gather.6.cloned.1.call-update) | async-done | bytes 2097168 | tf_op jit(solution)/shard_map/all_gather | solution.py:36
  323.3 3.2 multiply_convert_fusion.4
  330.7 3.2 pad_maximum_fusion
  335.6 3.8 fusion.16
  339.4 5.7 copy.147
  345.3 8.9 %scatter_fusion = f32[128,32,128]{2,0,1:T(8,128)S(1)} fusion(f32[128,32,128]{2,0,1:T(8,128)S(1)} %broadcast_in_dim.11.clone, s32[64]{0:T(128)S(1)} %fusion.59, f32[64,128,128]{2,1,0:T(8,128)} %bitcast.113), kind=kCustom, calls=%fused_computation.3 | custom fusion | flops 1048576 | bytes 12583168 | tf_op jit(solution)/shard_map/scatter-add | solution.py:55
  354.2 1.2 convert_element_type.51
  355.9 4.3 fusion.12
  360.2 5.8 copy.159
  366.1 2.7 fusion.9
  368.8 5.7 copy.160
  374.4 7.9 %maximum_bitcast_fusion = f32[128,128,128]{2,1,0:T(8,128)} fusion(f32[128,64,128]{2,0,1:T(8,128)} %copy.160, f32[128,64,128]{2,0,1:T(8,128)} %copy.159), kind=kLoop, calls=%fused_computation.5 | loop fusion | flops 2097152 | bytes 16777216 | tf_op jit(solution)/shard_map/concatenate | solution.py:69
  382.6 17.1 %scatter_fusion.1 = f32[128,32,128]{2,0,1:T(8,128)S(1)} fusion(f32[128,32,128]{2,0,1:T(8,128)S(1)} %broadcast_in_dim.11.clone.1, s32[128]{0:T(128)S(1)} %fusion.60, f32[128,128,128]{2,1,0:T(8,128)} %maximum_bitcast_fusion), kind=kCustom, calls=%fused_computation.4 | custom fusion | flops 2097152 | bytes 25166336 | tf_op jit(solution)/shard_map/scatter-add | solution.py:72
  401.6 102.0 %all-reduce.6.cloned.1.call-done = bf16[16,3,4,128,128]{4,3,2,0,1:T(8,128)(2,1)} async-done(((bf16[16,3,4,128,128]{4,3,2,0,1:T(8,128)(2,1)}), bf16[16,3,4,128,128]{4,3,2,0,1:T(8,128)(2,1)}) %all-reduce.6.cloned.1.call-update) | async-done | bytes 6291472
  503.6 2.4 constant_dynamic-slice_fusion
  506.1 77.5 %reduce-scatter.6.cloned.1.call-done = bf16[128,4,128]{2,0,1:T(8,128)(2,1)} async-done(((bf16[128,32,128]{2,0,1:T(8,128)(2,1)}), bf16[128,4,128]{2,0,1:T(8,128)(2,1)}) %reduce-scatter.6.cloned.1.call-update) | async-done | bytes 131088 | tf_op jit(solution)/shard_map/reduce_scatter | solution.py:75
  585.4 78.5 %reduce-scatter.8.cloned.1.call-done = bf16[128,4,128]{2,0,1:T(8,128)(2,1)} async-done(((bf16[128,32,128]{2,0,1:T(8,128)(2,1)}), bf16[128,4,128]{2,0,1:T(8,128)(2,1)}) %reduce-scatter.8.cloned.1.call-update) | async-done | bytes 131088 | tf_op jit(solution)/shard_map/reduce_scatter | solution.py:78
  665.7 31.9 %all-reduce.4.cloned.1.call-done = bf16[1,3,4,128,128]{4,3,2,0,1:T(8,128)(2,1)} async-done(((bf16[1,3,4,128,128]{4,3,2,0,1:T(8,128)(2,1)}), bf16[1,3,4,128,128]{4,3,2,0,1:T(8,128)(2,1)}) %all-reduce.4.cloned.1.call-update) | async-done | bytes 393232 | tf_op jit(solution)/shard_map/psum | solution.py:102
  (81 shorter events, 20.8 us)
Async XLA Ops:
  7.2 57.9 %all-gather.10.cloned.1.call-start = ((), (), s32[]{:S(2)}) async-start(), calls=%async_computation.4 | async-start | bytes 1179648 | tf_op jit(solution)/shard_map/all_gather | solution.py:19
  8.9 109.6 %all-gather.14.cloned.1.call-start = ((), (), s32[]{:S(2)}) async-start(), calls=%async_computation.7 | async-start | bytes 1179648 | tf_op jit(solution)/shard_map/all_gather | solution.py:20
  10.6 171.8 %all-gather.8.cloned.1.call-start = ((), (), s32[]{:S(2)}) async-start(), calls=%async_computation.3 | async-start | bytes 2228224 | tf_op jit(solution)/shard_map/all_gather | solution.py:34
  11.4 241.5 %all-gather.12.cloned.1.call-start = ((), (), s32[]{:S(2)}) async-start(), calls=%async_computation.5 | async-start | bytes 2228224 | tf_op jit(solution)/shard_map/all_gather | solution.py:35
  12.0 311.4 %all-gather.6.cloned.1.call-start = ((), (), s32[]{:S(2)}) async-start(), calls=%async_computation.2 | async-start | bytes 2228224 | tf_op jit(solution)/shard_map/all_gather | solution.py:36
  12.5 491.1 %all-reduce.6.cloned.1.call-start = ((), (), s32[]{:S(2)}) async-start(), calls=%async_computation.10 | async-start | bytes 12582912
  186.6 136.7 %copy-start.2 = (bf16[16,4,128,128]{2,3,1,0:T(8,128)(2,1)S(1)}, bf16[16,4,128,128]{2,3,1,0:T(8,128)(2,1)}, u32[]{:S(2)}) copy-start(bf16[16,4,128,128]{2,3,1,0:T(8,128)(2,1)} %copy.155) | copy-start | bytes 6291460
  326.6 0.8 copy-start.5
  326.6 1.8 copy-start.3
  328.4 1.6 copy-start.4
  334.0 1.6 copy-start.1
  334.0 249.5 %reduce-scatter.6.cloned.1.call-start = ((), (), s32[]{:S(2)}) async-start(), calls=%async_computation.6 | async-start | bytes 1179648 | tf_op jit(solution)/shard_map/reduce_scatter | solution.py:75
  355.4 308.4 %reduce-scatter.8.cloned.1.call-start = ((), (), s32[]{:S(2)}) async-start(), calls=%async_computation.8 | async-start | bytes 1179648 | tf_op jit(solution)/shard_map/reduce_scatter | solution.py:78
  360.2 5.9 copy-start
  399.7 1.2 copy-start.6
  400.9 296.6 %all-reduce.4.cloned.1.call-start = ((), (), s32[]{:S(2)}) async-start(), calls=%async_computation.9 | async-start | bytes 786432 | tf_op jit(solution)/shard_map/psum | solution.py:102
Sparse Core Ops, SparseCore 0:
  11.2 53.7 all-gather.9
  68.2 50.2 all-gather.13
  120.3 62.1 all-gather.7
  184.1 68.7 all-gather.11
  254.6 68.7 all-gather.5
  334.1 169.4 all-reduce.5
  507.5 76.0 reduce-scatter.5
  587.9 75.8 reduce-scatter.7
  666.5 31.0 all-reduce.3
where the time goes:
time: 707 us; the launch traced here: 706 us
  waiting for transfers between devices  575 us (81%)
  local copies, waits for them, and re-layouts  49.7 us (7%)
  other arithmetic  42.3 us (6%)
  matrix products  24.8 us (4%)
  between operations  14.1 us (2%)
    unnamed x10, waiting for transfers between devices  104 us
    reduce_scatter x1, waiting for transfers between devices, per_device(): lax.psum_scatter(in_acc.astype(jnp.bfloat16), 'row', scatter_dimension=1,...  78.5 us
    reduce_scatter x1, waiting for transfers between devices, per_device(): lax.psum_scatter(out_acc.astype(jnp.bfloat16), 'row', scatter_dimension=1...  77.5 us
    all_gather x1, waiting for transfers between devices, per_device(): w_up = lax.all_gather(up_blocks, 'col', axis=0, tiled=True)  66.3 us
    all_gather x1, waiting for transfers between devices, per_device(): w_down = lax.all_gather(down_blocks, 'col', axis=0, tiled=True)  66.2 us
    all_gather x1, waiting for transfers between devices, per_device(): lax.all_gather(cotangent, 'row', axis=1, tiled=True)  51.9 us
    all_gather x1, waiting for transfers between devices, per_device(): lax.all_gather(tokens, 'row', axis=1, tiled=True)  49.4 us
    all_gather x1, waiting for transfers between devices, per_device(): w_gate = lax.all_gather(gate_blocks, 'col', axis=0, tiled=True)  49.1 us
  transfers between devices with their start and end apart: 9, of which 9 were waited for; matrix products, arithmetic and copies ran while one was open for 14% of the time, Pallas kernels for 0%

commit v1 on v0

v1 whole, which is shorter than its diff:
```python
import jax
import jax.numpy as jnp
from jax import lax
from jax.experimental import pallas as pl
from jax.experimental.pallas import tpu as pltpu
from jax.sharding import PartitionSpec as P

BLK = 128
SLOTS = 4
GROUP = 8
NBLK = 32
F32 = jnp.float32
BF16 = jnp.bfloat16
MESH = pl.DeviceIdType.MESH

T_GATE, T_UP, T_DOWN, T_PREV_OUT, T_LAST_OUT, T_PREV_IN, T_LAST_IN = 0, 32, 64, 96, 128, 160, 224


def dot(a, b, dims):
    return lax.dot_general(a, b, (dims, ((), ())), preferred_element_type=F32)


def block_of(ref, place):
    return ref[place // 8, (place // 2) % 4, place % 2]


class Copies:
    def __init__(self, send_sem, recv_sem, neighbours):
        self.send_sem, self.recv_sem, self.neighbours = send_sem, recv_sem, neighbours
        self.made = {}

    def send(self, name, src, dst, way):
        number = len(self.made)
        copy = pltpu.make_async_remote_copy(
            src_ref=src,
            dst_ref=dst,
            send_sem=self.send_sem.at[number],
            recv_sem=self.recv_sem.at[number],
            device_id=self.neighbours[way],
            device_id_type=MESH,
        )
        copy.start()
        self.made[name] = copy

    def recv(self, name):
        self.made[name].wait_recv()

    def finish(self):
        for copy in self.made.values():
            copy.wait_send()


def add_into(dst, srcs, dims, rows=64):
    total = 1
    for size in dims[:-2]:
        total *= size
    per = dims[-2] // rows

    def body(i, _):
        index = []
        rest = i // per
        for size in reversed(dims[:-2]):
            index.insert(0, rest % size)
            rest = rest // size
        index = tuple(index) + (pl.ds(pl.multiple_of((i % per) * rows, rows), rows),)
        value = dst[index].astype(F32)
        for src in srcs:
            value = value + src[index].astype(F32)
        dst[index] = value.astype(dst.dtype)
        return 0

    lax.fori_loop(0, total * per, body, 0)


def kernel(
    table, tokens, cotangent, gate_blocks, up_blocks, down_blocks,
    out_ref, in_ref, gate_grad, up_grad, down_grad,
    xt, xc, w, s_out, s_in, act_s, gd_s, ud_s, b_out, b_in, grads,
    ra, rb, qa, qb, g_sib, rz_half, rz,
    local_sem, send_sem, recv_sem,
):
    core = lax.axis_index("dp")
    row = lax.axis_index("row")
    col = lax.axis_index("col")
    y, xh, xl, z = row // 2, row % 2, col // 8, col % 8
    x = xh * 2 + xl

    def at(core=core, x=x, y=y, z=z):
        return (core, y * 2 + x // 2, (x % 2) * 8 + z)

    xs = [(x + o) % 4 for o in range(4)]
    ys = [(y + o) % 4 for o in range(4)]
    zs = [(z + o) % 8 for o in range(8)]
    ways = {
        "x+": at(x=xs[1]), "x-": at(x=xs[3]), "y+": at(y=ys[1]), "y-": at(y=ys[3]),
        "z+": at(z=zs[1]), "z-": at(z=zs[7]), "c": at(core=1 - core),
    }
    cp = Copies(send_sem, recv_sem, ways)

    barrier = pltpu.get_barrier_semaphore()
    for way in ways.values():
        pl.semaphore_signal(barrier, inc=1, device_id=way, device_id_type=MESH)

    def half(x_):
        return pl.ds(pl.multiple_of((x_ % 2) * 128, 128), 128)

    local = []

    def copy_in(src, dst):
        copy = pltpu.make_async_copy(src, dst, local_sem.at[len(local)])
        copy.start()
        local.append(copy)

    for src, dst in ((tokens, xt), (cotangent, xc)):
        for hj in range(4):
            copy_in(src.at[:, pl.ds(hj * BLK, BLK)], dst.at[hj, y, xh, half(x)])
    for i, src in enumerate((gate_blocks, up_blocks, down_blocks)):
        copy_in(src.at[0], w.at[i, z])
    zero = jnp.zeros((256, BLK), BF16)
    xt[4, 0, 0] = zero
    xc[4, 0, 0] = zero
    s_out[NBLK] = jnp.zeros((256, BLK), F32)
    s_in[2 * NBLK] = jnp.zeros((256, BLK), F32)
    for copy in local:
        copy.wait()
    pl.semaphore_wait(barrier, len(ways))

    def piece(ref, hj, n, y_, x_):
        return ref.at[pl.ds(hj, n), y_, x_ // 2, half(x_)]

    def line_x(ref, hj, y_):
        return ref.at[hj, y_]

    def line_y(ref, hj, x_):
        return ref.at[hj, :, x_ // 2, half(x_)]

    def send_same(name, ref, way):
        cp.send(name, ref, ref, way)

    def gather_a(t, ref):
        for way in ("x+", "x-"):
            send_same((t, "a", way), piece(ref, 0, 2, y, x), way)
        for way in ("y+", "y-"):
            send_same((t, "a", way), piece(ref, 2, 2, y, x), way)

    def gather_b(t, ref):
        cp.recv((t, "a", "x+"))
        send_same((t, "b", "x+"), piece(ref, 0, 1, y, xs[3]), "x+")
        cp.recv((t, "a", "x-"))
        send_same((t, "b", "x-"), piece(ref, 1, 1, y, xs[1]), "x-")
        cp.recv((t, "a", "y+"))
        send_same((t, "b", "y+"), piece(ref, 2, 1, ys[3], x), "y+")
        cp.recv((t, "a", "y-"))
        send_same((t, "b", "y-"), piece(ref, 3, 1, ys[1], x), "y-")

    def gather_c(t, ref):
        cp.recv((t, "b", "x+"))
        cp.recv((t, "b", "x-"))
        for hj, way in ((0, "y+"), (1, "y-"), (1, "y+"), (0, "y-")):
            send_same((t, "c", way, hj), line_x(ref, hj, y), way)
        cp.recv((t, "b", "y+"))
        cp.recv((t, "b", "y-"))
        for hj, way in ((2, "x+"), (3, "x-"), (3, "x+"), (2, "x-")):
            send_same((t, "c", way, hj), line_y(ref, hj, x), way)

    def gather_d(t, ref):
        cp.recv((t, "c", "y+", 0))
        send_same((t, "d", "y+"), line_x(ref, 0, ys[3]), "y+")
        cp.recv((t, "c", "y-", 1))
        send_same((t, "d", "y-"), line_x(ref, 1, ys[1]), "y-")
        cp.recv((t, "c", "x+", 2))
        send_same((t, "d", "x+"), line_y(ref, 2, xs[3]), "x+")
        cp.recv((t, "c", "x-", 3))
        send_same((t, "d", "x-"), line_y(ref, 3, xs[1]), "x-")

    def gather_end(t):
        for hj, way in ((1, "y+"), (0, "y-"), (3, "x+"), (2, "x-")):
            cp.recv((t, "c", way, hj))
        for way in ("y+", "y-", "x+", "x-"):
            cp.recv((t, "d", way))

    mine = core * 2

    def w_piece(o, first=0, n=2):
        return w.at[:, zs[o % 8], pl.ds(mine + first, n)]

    def weights_first():
        send_same(("w", 1, "z+"), w_piece(0), "z+")
        send_same(("w", 1, "z-"), w_piece(0), "z-")

    def weights_step(k):
        cp.recv(("w", k, "z+"))
        if k < 3:
            send_same(("w", k + 1, "z+"), w_piece(-k), "z+")
        if k == 3:
            send_same(("w", 4, "z+"), w_piece(-3, 0, 1), "z+")
        cp.recv(("w", k, "z-"))
        if k < 3:
            send_same(("w", k + 1, "z-"), w_piece(k), "z-")
        if k == 3:
            send_same(("w", 4, "z-"), w_piece(3, 1, 1), "z-")
        send_same(("ws", k), w_piece(-k), "c")
        if k < 4:
            send_same(("ws", -k), w_piece(k), "c")

    def weights_end():
        for k in (1, 2, 3, 4, -1, -2, -3):
            cp.recv(("ws", k))

    gather_a("t", xt)
    gather_a("c", xc)
    weights_first()
    gather_b("t", xt)
    gather_b("c", xc)
    gather_c("t", xt)
    weights_step(1)
    gather_c("c", xc)
    gather_d("t", xt)
    weights_step(2)
    weights_step(3)
    gather_end("t")
    gather_d("c", xc)
    weights_step(4)
    weights_end()
    gather_end("c")

    def picked(ref, first, p):
        return jnp.concatenate(
            [block_of(ref, table[first + p * SLOTS + s]) for s in range(SLOTS)], axis=1
        )

    def w_rows(i, p):
        return w[i, p].reshape(SLOTS * BLK, BLK)

    def w_lanes(i, p):
        return jnp.concatenate([w[i, p, s] for s in range(SLOTS)], axis=1)

    def forward(p, _):
        gate = dot(picked(xt, T_GATE, p), w_rows(0, p), ((1,), (0,)))
        up = dot(picked(xt, T_UP, p), w_rows(1, p), ((1,), (0,)))
        sig = jax.nn.sigmoid(gate)
        swish = gate * sig
        act = (swish * up).astype(BF16)
        act_s[p] = act
        wd = w_lanes(2, p)
        spread = dot(act, wd, ((1,), (0,)))
        for s in range(SLOTS):
            e = p * SLOTS + s
            s_out[e] = s_out[table[T_PREV_OUT + e]] + spread[:, s * BLK:(s + 1) * BLK]
        act_grad = dot(picked(xc, T_DOWN, p), wd, ((1,), (1,)))
        slope = sig * (1.0 + gate * (1.0 - sig))
        gd_s[p] = (act_grad * up * slope).astype(BF16)
        ud_s[p] = (act_grad * swish).astype(BF16)
        return 0

    lax.fori_loop(0, GROUP, forward, 0)

    def collect(dst, src, first):
        def body(q, _):
            dst[q // 8, (q // 2) % 4, q % 2] = src[table[first + q]].astype(BF16)
            return 0

        lax.fori_loop(0, NBLK, body, 0)

    def stage(t, name, axis, hj, part, bufs, dims):
        near = xs if axis == "x" else ys
        plus, minus = axis + "+", axis + "-"
        b1, b2, b3 = bufs

        def first():
            cp.send((t, name, 1, plus), part(hj, near[2]), b1.at[0], plus)
            cp.send((t, name, 1, minus), part(hj + 1, near[2]), b1.at[1], minus)
            cp.send((t, name, 2, plus), part(hj + 1, near[1]), b2.at[0], plus)
            cp.send((t, name, 2, minus), part(hj, near[3]), b2.at[1], minus)

        def second():
            cp.recv((t, name, 1, plus))
            add_into(part(hj, near[1]), [b1.at[0]], dims)
            cp.send((t, name, 3, plus), part(hj, near[1]), b3.at[0], plus)
            cp.recv((t, name, 1, minus))
            add_into(part(hj + 1, near[3]), [b1.at[1]], dims)
            cp.send((t, name, 3, minus), part(hj + 1, near[3]), b3.at[1], minus)

        def third():
            cp.recv((t, name, 2, plus))
            cp.recv((t, name, 2, minus))
            cp.recv((t, name, 3, plus))
            add_into(part(hj, near[0]), [b3.at[0], b2.at[1]], dims)
            cp.recv((t, name, 3, minus))
            add_into(part(hj + 1, near[0]), [b2.at[0], b3.at[1]], dims)

        return first, second, third

    def reduce_of(k, t, ref):
        def along_x(hj, y_):
            return ref.at[hj, y_]

        def along_y(hj, x_):
            return ref.at[hj, :, x_ // 2, half(x_)]

        def end_x(hj, x_):
            return ref.at[hj, y, x_ // 2, half(x_)]

        def end_y(hj, y_):
            return ref.at[hj, y_, xh, half(x)]

        y1 = stage(t, "y1", "y", 0, along_x, [ra.at[k, i] for i in range(3)], (2, 256, BLK))
        x1 = stage(t, "x1", "x", 2, along_y, [rb.at[k, i] for i in range(3)], (4, 128, BLK))
        x2 = stage(t, "x2", "x", 0, end_x, [qa.at[k, i] for i in range(3)], (128, BLK))
        y2 = stage(t, "y2", "y", 2, end_y, [qb.at[k, i] for i in range(3)], (128, BLK))
        return y1, x1, x2, y2

    o_y1, o_x1, o_x2, o_y2 = reduce_of(0, "o", b_out)
    i_y1, i_x1, i_x2, i_y2 = reduce_of(1, "i", b_in)

    collect(b_out, s_out, T_LAST_OUT)
    o_y1[0]()
    o_x1[0]()

    def backward(p, _):
        for i, delta in ((0, gd_s), (1, ud_s)):
            back = dot(delta[p], w_rows(i, p), ((1,), (1,)))
            for s in range(SLOTS):
                e = p * 8 + i * SLOTS + s
                s_in[e] = s_in[table[T_PREV_IN + e]] + back[:, s * BLK:(s + 1) * BLK]
        return 0

    lax.fori_loop(0, GROUP, backward, 0)
    collect(b_in, s_in, T_LAST_IN)
    o_y1[1]()
    o_x1[1]()
    i_y1[0]()
    i_x1[0]()

    def down_term(p, _):
        term = dot(act_s[p], picked(xc, T_DOWN, p), ((0,), (0,)))
        for s in range(SLOTS):
            grads[2, p, s] = term[:, s * BLK:(s + 1) * BLK].astype(BF16)
        return 0

    def in_term(i, first, delta):
        def body(p, _):
            term = dot(picked(xt, first, p), delta[p], ((0,), (0,)))
            grads[i, p] = term.astype(BF16).reshape(SLOTS, BLK, BLK)
            return 0

        return body

    theirs = (1 - core) * 2

    def sibling(i):
        cp.send(("gs", i), grads.at[i, :, pl.ds(theirs, 2)], g_sib.at[i], "c")

    lax.fori_loop(0, GROUP, down_term, 0)
    sibling(2)
    lax.fori_loop(0, GROUP, in_term(0, T_GATE, gd_s), 0)
    sibling(0)
    lax.fori_loop(0, GROUP, in_term(1, T_UP, ud_s), 0)
    sibling(1)

    def g_part(i, o, first=0, n=2):
        return grads.at[i, zs[o % 8], pl.ds(mine + first, n)]

    def z_first(i):
        cp.recv(("gs", i))
        add_into(grads.at[i, :, pl.ds(mine, 2)], [g_sib.at[i]], (8, 2, 128, BLK))
        cp.send(("z", i, 1, "z+"), g_part(i, 4, 0, 1), rz_half.at[i, pl.ds(0, 1)], "z+")
        cp.send(("z", i, 1, "z-"), g_part(i, 4, 1, 1), rz_half.at[i, pl.ds(1, 1)], "z-")

    def z_step(i, k):
        cp.recv(("z", i, k, "z+"))
        o = 4 - k
        if k == 1:
            add_into(g_part(i, o, 0, 1), [rz_half.at[i, pl.ds(0, 1)]], (1, 128, BLK))
        else:
            add_into(g_part(i, o), [rz.at[i, k - 2, 0]], (2, 128, BLK))
        cp.send(("z", i, k + 1, "z+"), g_part(i, o), rz.at[i, k - 1, 0], "z+")
        cp.recv(("z", i, k, "z-"))
        if k == 1:
            add_into(g_part(i, -o, 1, 1), [rz_half.at[i, pl.ds(1, 1)]], (1, 128, BLK))
        else:
            add_into(g_part(i, -o), [rz.at[i, k - 2, 1]], (2, 128, BLK))
        cp.send(("z", i, k + 1, "z-"), g_part(i, -o), rz.at[i, k - 1, 1], "z-")

    grad_refs = (gate_grad, up_grad, down_grad)

    def z_last(i):
        cp.recv(("z", i, 4, "z+"))
        cp.recv(("z", i, 4, "z-"))
        ref = grad_refs[i]

        def body(n, _):
            rows = pl.ds(pl.multiple_of((n % 2) * 64, 64), 64)
            s = n // 2
            ref[0, mine + s, rows] = (
                grads[i, z, mine + s, rows].astype(F32)
                + rz[i, 2, 0, s, rows].astype(F32)
                + rz[i, 2, 1, s, rows].astype(F32)
            )
            return 0

        lax.fori_loop(0, 4, body, 0)
        part = ref.at[0, pl.ds(mine, 2)]
        cp.send(("gf", i), part, part, "c")

    order = (2, 0, 1)
    z_first(2)
    z_first(0)
    z_first(1)
    o_y1[2]()
    o_x2[0]()
    o_x1[2]()
    o_y2[0]()
    for i in order:
        z_step(i, 1)
    o_x2[1]()
    o_y2[1]()
    i_y1[1]()
    i_x1[1]()
    for i in order:
        z_step(i, 2)
    o_x2[2]()
    o_y2[2]()
    i_y1[2]()
    i_x2[0]()
    i_x1[2]()
    i_y2[0]()
    for i in order:
        z_step(i, 3)
    i_x2[1]()
    i_y2[1]()
    for i in order:
        z_last(i)
    i_x2[2]()
    i_y2[2]()

    for hj in range(4):
        out_ref[:, hj * BLK:(hj + 1) * BLK] = b_out[hj, y, xh, half(x)]
        in_ref[:, hj * BLK:(hj + 1) * BLK] = b_in[hj, y, xh, half(x)]
    for i in order:
        cp.recv(("gf", i))
    cp.finish()


def chain(keys, count):
    number = jnp.arange(count, dtype=jnp.int32)
    same = (keys[:, None] == keys[None, :]) & (number[None, :] < number[:, None])
    prev = jnp.max(jnp.where(same, number[None, :], -1), axis=1)
    places = jnp.arange(NBLK, dtype=jnp.int32)
    last = jnp.max(jnp.where(keys[None, :] == places[:, None], number[None, :], -1), axis=1)
    return jnp.where(prev < 0, count, prev), jnp.where(last < 0, count, last)


def per_device(
    tokens, cotangent, gate_blocks, up_blocks, down_blocks, gate_index, up_index, down_index
):
    line = (lax.axis_index("row") * 2 + lax.axis_index("col") // GROUP) * GROUP

    def places(index):
        mine = lax.dynamic_slice_in_dim(index, line, GROUP, 0)
        return jnp.where(mine < NBLK, (mine % 4) * 8 + mine // 4, NBLK).astype(jnp.int32)

    gate, up, down = places(gate_index), places(up_index), places(down_index)
    prev_out, last_out = chain(down.reshape(-1), NBLK)
    prev_in, last_in = chain(jnp.concatenate((gate, up), axis=1).reshape(-1), 2 * NBLK)
    table = jnp.concatenate(
        (gate.reshape(-1), up.reshape(-1), down.reshape(-1), prev_out, last_out, prev_in, last_in)
    )
    any_spec = pl.BlockSpec(memory_space=pl.ANY)
    vmem_spec = pl.BlockSpec(memory_space=pltpu.VMEM)
    grad = jax.ShapeDtypeStruct((1, SLOTS, BLK, BLK), F32)
    act = jax.ShapeDtypeStruct((128, 4 * BLK), BF16)
    big = (4, 4, 2, 256, BLK)
    count = 140
    return pl.pallas_call(
        kernel,
        out_shape=(act, act, grad, grad, grad),
        in_specs=[pl.BlockSpec(memory_space=pltpu.SMEM)] + [any_spec] * 5,
        out_specs=(vmem_spec,) * 5,
        scratch_shapes=[
            pltpu.VMEM((5, 4, 2, 256, BLK), BF16),
            pltpu.VMEM((5, 4, 2, 256, BLK), BF16),
            pltpu.VMEM((3, GROUP, SLOTS, BLK, BLK), BF16),
            pltpu.VMEM((NBLK + 1, 256, BLK), F32),
            pltpu.VMEM((2 * NBLK + 1, 256, BLK), F32),
            pltpu.VMEM((GROUP, 256, BLK), BF16),
            pltpu.VMEM((GROUP, 256, BLK), BF16),
            pltpu.VMEM((GROUP, 256, BLK), BF16),
            pltpu.VMEM(big, BF16),
            pltpu.VMEM(big, BF16),
            pltpu.VMEM((3, GROUP, SLOTS, BLK, BLK), BF16),
            pltpu.VMEM((2, 3, 2, 2, 256, BLK), BF16),
            pltpu.VMEM((2, 3, 2, 4, 128, BLK), BF16),
            pltpu.VMEM((2, 3, 2, 128, BLK), BF16),
            pltpu.VMEM((2, 3, 2, 128, BLK), BF16),
            pltpu.VMEM((3, GROUP, 2, BLK, BLK), BF16),
            pltpu.VMEM((3, 2, BLK, BLK), BF16),
            pltpu.VMEM((3, 3, 2, 2, BLK, BLK), BF16),
            pltpu.SemaphoreType.DMA((11,)),
            pltpu.SemaphoreType.DMA((count,)),
            pltpu.SemaphoreType.DMA((count,)),
        ],
        compiler_params=pltpu.CompilerParams(
            collective_id=0, has_side_effects=True, vmem_limit_bytes=56 << 20
        ),
        name="ffn",
    )(table, tokens, cotangent, gate_blocks, up_blocks, down_blocks)


def solution(mesh):
    act = P(("dp", "col"), "row")
    blocks = P(("row", "col"), None, None, None)
    return jax.shard_map(
        per_device,
        mesh=mesh,
        in_specs=(act, act, blocks, blocks, blocks, P(), P(), P()),
        out_specs=(act, act, blocks, blocks, blocks),
        check_vma=False,
    )
```

time: 707 us -> 89.9 us (0.13)
  waiting for transfers between devices: 575 us -> 0 us
  Pallas kernels: 0 us -> 79.9 us
  other arithmetic: 42.3 us -> 0.75 us
  local copies, waits for them, and re-layouts: 49.7 us -> 8.24 us
  matrix products: 24.8 us -> 0 us
  between operations: 14.1 us -> 0.74 us
    all_gather x5 -> x0, waiting for transfers between devices: 283 us -> none  [the longest x1 66.3 us: per_device(): w_up = lax.all_gather(up_blocks, 'col', axis=0, tiled=True)]
    reduce_scatter x2 -> x0, waiting for transfers between devices: 156 us -> none  [the longest x1 78.5 us: per_device(): lax.psum_scatter(in_acc.astype(jnp.bfloat16), 'row', scatter_dimension=1,...]
    unnamed x10 -> x0, waiting for transfers between devices: 104 us -> none
    pallas_call x0 -> x1, Pallas kernels: none -> 79.9 us  [per_device(): pl.pallas_call(kernel, out_shape=(act, act, grad, grad, grad), in_specs=[...]
    psum x1 -> x0, waiting for transfers between devices: 31.9 us -> none  [per_device(): grad_total = lax.psum(owned_sum, 'dp').astype(jnp.float32)]
    scatter-add x2 -> x0, other arithmetic: 26.1 us -> none  [the longest x1 17.1 us: per_device(): in_acc = in_acc.at[:, in_target].add(in_terms)]
    dot_general x9 -> x0, matrix products: 24.8 us -> none  [the longest x1 4.3 us: per_device(): jnp.einsum('tno,nsbo->tnsb', gate_delta, w_gate, preferred_element_type=j...]
    reshape x6 -> x3, local copies, waits for them, and re-layouts: 20.5 us -> 0.24 us  [the longest x1 0.08 us: per_device(): down.reshape(-1)]
  transfers between devices with their start and end apart: 9 -> 0, of which waited for: 9 -> 0; matrix products, arithmetic and copies ran while one was open for 14% -> 0% of each run, Pallas kernels for 0% -> 0%
where the time goes in v1:
time: 89.9 us; the launch traced here: 89.6 us
  Pallas kernels  79.9 us (89%)
  local copies, waits for them, and re-layouts  8.24 us (9%)
    pallas_call x1, Pallas kernels, per_device(): pl.pallas_call(kernel, out_shape=(act, act, grad, grad, grad), in_specs=[...  79.9 us
    unnamed x19, local copies, waits for them, and re-layouts  6.94 us

profile of v1, /device:TPU:1, one launch (start us, length us, event | category | flops | bytes accessed | tf_op | source)
XLA Modules:
  0.0 89.6 jit_solution(2440661451052044220)
XLA Ops:
  0.6 0.0 copy-start.4
  0.7 0.7 copy-done.4
  1.3 0.0 copy-start.5
  1.3 0.1 fusion.4
  1.4 0.6 copy-done.5
  2.0 0.1 fusion.7
  2.1 0.6 copy-done.6
  2.7 0.1 fusion.10
  2.8 0.1 copy.23
  2.9 0.1 reshape.25
  2.9 0.2 select_reduce_fusion.2
  3.2 0.1 copy.24
  3.2 0.1 eq.58
  3.3 0.2 select_reduce_fusion
  3.5 0.1 select_reduce_fusion.1
  3.6 0.1 copy.21
  3.7 0.1 reshape.23
  3.8 0.1 copy.22
  3.9 0.1 reshape.24
  4.0 0.7 concatenate.7.table
  4.6 79.9 %ffn.1 = (bf16[128,512]{1,0:T(8,128)(2,1)}, bf16[128,512]{1,0:T(8,128)(2,1)}, f32[1,4,128,128]{3,2,1,0:T(8,128)}, f32[1,4,128,128]{3,2,1,0:T(8,128)}, f32[1,4,128,128]{3,2,1,0:T(8,128)}) custom-call(s32[256]{0:T(256)} %concatenate.7.table, bf16[128,512]{1,0:T(8,128)(2,1)} %tokens.1, bf16[128,512]{1,0:T(8,128)(2,1)} %cotangent.1, ...), custom_call_target="tpu_custom_call" | custom-call | tf_op jit(solution)/shard_map/ffn/pallas_call | solution.py:475
  84.5 0.0 copy-start.3
  84.5 0.0 copy-start.2
  84.5 1.6 %copy.30 = bf16[128,512]{1,0:T(8,128)(2,1)} copy(bf16[128,512]{1,0:T(8,128)(2,1)} %get-tuple-element.14) | data formatting | bytes 262144
  86.1 0.0 copy-done.3
  86.1 0.7 copy.31
  86.8 0.0 copy-done.2
  86.8 0.7 copy.32
  87.5 0.3 copy-done.1
  87.8 0.7 copy.33
  88.5 0.3 copy-done
  88.9 0.7 copy.34
  (7 shorter events, 0.0 us)
Async XLA Ops:
  0.6 0.7 copy-start.4
  1.3 0.7 copy-start.5
  2.0 0.7 copy-start.6
  84.5 1.6 %copy-start.3 = (bf16[128,512]{1,0:T(8,128)(2,1)S(1)}, bf16[128,512]{1,0:T(8,128)(2,1)}, u32[]{:S(2)}) copy-start(bf16[128,512]{1,0:T(8,128)(2,1)} %get-tuple-element.15) | copy-start | bytes 393220
  84.5 2.3 %copy-start.2 = (f32[1,4,128,128]{3,2,1,0:T(8,128)S(1)}, f32[1,4,128,128]{3,2,1,0:T(8,128)}, u32[]{:S(2)}) copy-start(f32[1,4,128,128]{3,2,1,0:T(8,128)} %get-tuple-element.16) | copy-start | bytes 786436
  86.8 1.0 %copy-start.1 = (f32[1,4,128,128]{3,2,1,0:T(8,128)S(1)}, f32[1,4,128,128]{3,2,1,0:T(8,128)}, u32[]{:S(2)}) copy-start(f32[1,4,128,128]{3,2,1,0:T(8,128)} %get-tuple-element.17) | copy-start | bytes 786436
  87.8 1.0 %copy-start = (f32[1,4,128,128]{3,2,1,0:T(8,128)S(1)}, f32[1,4,128,128]{3,2,1,0:T(8,128)}, u32[]{:S(2)}) copy-start(f32[1,4,128,128]{3,2,1,0:T(8,128)} %get-tuple-element.18) | copy-start | bytes 786436

commit v2 on v1

v2 whole, which is shorter than its diff:
```python
import jax
import jax.numpy as jnp
from jax import lax
from jax.experimental import pallas as pl
from jax.experimental.pallas import tpu as pltpu
from jax.sharding import PartitionSpec as P

BLK = 128
SLOTS = 4
GROUP = 8
NBLK = 32
F32 = jnp.float32
BF16 = jnp.bfloat16
MESH = pl.DeviceIdType.MESH

T_GATE, T_UP, T_DOWN, T_PREV_OUT, T_PREV_GATE, T_PREV_UP, T_LAST_OUT, T_LAST_IN = 0, 4, 8, 12, 16, 20, 24, 56
T_ROWS = 88
I32 = jnp.int32


def dot(a, b, dims):
    return lax.dot_general(a, b, (dims, ((), ())), preferred_element_type=F32)


def block_of(ref, place):
    return ref[place // 8, (place // 2) % 4, place % 2]


class Copies:
    def __init__(self, send_sem, recv_sem, neighbours):
        self.send_sem, self.recv_sem, self.neighbours = send_sem, recv_sem, neighbours
        self.made = {}

    def send(self, name, src, dst, way):
        number = len(self.made)
        copy = pltpu.make_async_remote_copy(
            src_ref=src,
            dst_ref=dst,
            send_sem=self.send_sem.at[number],
            recv_sem=self.recv_sem.at[number],
            device_id=self.neighbours[way],
            device_id_type=MESH,
        )
        copy.start()
        self.made[name] = copy

    def recv(self, name):
        self.made[name].wait_recv()

    def finish(self):
        for copy in self.made.values():
            copy.wait_send()


def add_into(dst, srcs, dims, rows=64):
    total = 1
    for size in dims[:-2]:
        total *= size
    per = dims[-2] // rows

    def body(i, _):
        index = []
        rest = i // per
        for size in reversed(dims[:-2]):
            index.insert(0, rest % size)
            rest = rest // size
        index = tuple(index) + (pl.ds(pl.multiple_of((i % per) * rows, rows), rows),)
        value = dst[index].astype(F32)
        for src in srcs:
            value = value + src[index].astype(F32)
        dst[index] = value.astype(dst.dtype)
        return 0

    lax.fori_loop(0, total * per, body, 0)


def make_table(keys, tab, first):
    lane = lax.broadcasted_iota(I32, (SLOTS, BLK), 1)
    panel = lane & 7

    def place(v):
        return jnp.where(v < NBLK, (v & 3) * 8 + (v >> 2), NBLK)

    gate, up, down = (place(keys[i]) for i in range(3))
    tab[T_GATE:T_GATE + SLOTS] = gate
    tab[T_UP:T_UP + SLOTS] = up
    tab[T_DOWN:T_DOWN + SLOTS] = down

    prev_out = jnp.full((SLOTS, BLK), NBLK, I32)
    prev_gate = jnp.full((SLOTS, BLK), 2 * NBLK, I32)
    prev_up = prev_gate
    for d in range(GROUP - 1, -1, -1):
        far = panel >= d
        if d:
            moved = pltpu.roll(down, d, axis=1)
            for s in range(SLOTS):
                hit = (down == moved[s:s + 1]) & far
                prev_out = jnp.where(hit, (panel - d) * SLOTS + s, prev_out)
        for i, src in enumerate((gate, up)):
            if d == 0 and i == 1:
                continue
            moved = pltpu.roll(src, d, axis=1) if d else src
            for s in range(SLOTS):
                number = (panel - d) * 8 + i * SLOTS + s
                if d:
                    prev_gate = jnp.where((gate == moved[s:s + 1]) & far, number, prev_gate)
                prev_up = jnp.where((up == moved[s:s + 1]) & far, number, prev_up)
    tab[T_PREV_OUT:T_PREV_OUT + SLOTS] = prev_out
    tab[T_PREV_GATE:T_PREV_GATE + SLOTS] = prev_gate
    tab[T_PREV_UP:T_PREV_UP + SLOTS] = prev_up

    wanted = lax.broadcasted_iota(I32, (NBLK, BLK), 0)
    ours = lax.broadcasted_iota(I32, (NBLK, BLK), 1) - first
    inside = (ours >= 0) & (ours < GROUP)

    def last(sources, per):
        best = jnp.full((NBLK, BLK), -1, I32)
        for i, src in enumerate(sources):
            for s in range(SLOTS):
                hit = (wanted == src[s:s + 1]) & inside
                best = jnp.maximum(best, jnp.where(hit, ours * per + i * SLOTS + s, -1))
        best = jnp.max(best, axis=1, keepdims=True)
        best = jnp.where(best < 0, per * GROUP, best)
        return jnp.broadcast_to(best, (NBLK, BLK))

    tab[T_LAST_OUT:T_LAST_OUT + NBLK] = last((down,), SLOTS)
    tab[T_LAST_IN:T_LAST_IN + NBLK] = last((gate, up), 2 * SLOTS)


def kernel(
    gate_index, up_index, down_index, tokens, cotangent, gate_blocks, up_blocks, down_blocks,
    out_ref, in_ref, grad_ref,
    keys, tab, table, xt, xc, turned, w, s_out, s_in, act_s, gd_s, ud_s, swish_s, slope_s,
    b_out, b_in, grads, ra, rb, qa, qb, g_sib, rz,
    key_sem, local_sem, send_sem, recv_sem,
):
    core = lax.axis_index("dp")
    row = lax.axis_index("row")
    col = lax.axis_index("col")
    y, xh, xl, z = row // 2, row % 2, col // 8, col % 8
    x = xh * 2 + xl

    def at(core=core, x=x, y=y, z=z):
        return (core, y * 2 + x // 2, (x % 2) * 8 + z)

    xs = [(x + o) % 4 for o in range(4)]
    ys = [(y + o) % 4 for o in range(4)]
    zs = [(z + o) % 8 for o in range(8)]
    ways = {
        "x+": at(x=xs[1]), "x-": at(x=xs[3]), "y+": at(y=ys[1]), "y-": at(y=ys[3]),
        "z+": at(z=zs[1]), "z-": at(z=zs[7]), "c": at(core=1 - core),
    }
    cp = Copies(send_sem, recv_sem, ways)

    barrier = pltpu.get_barrier_semaphore()
    for way in ways.values():
        pl.semaphore_signal(barrier, inc=1, device_id=way, device_id_type=MESH)

    def half(x_):
        return pl.ds(pl.multiple_of((x_ % 2) * 128, 128), 128)

    local = {}

    def copy_in(name, src, dst):
        copy = pltpu.make_async_copy(src, dst, local_sem.at[len(local)])
        copy.start()
        local[name] = copy

    for t, src, dst in (("t", tokens, xt), ("c", cotangent, xc)):
        for hj in range(4):
            copy_in((t, hj), src.at[:, pl.ds(hj * BLK, BLK)], dst.at[hj, y, xh, half(x)])
    for i, src in enumerate((gate_blocks, up_blocks, down_blocks)):
        copy_in(("w", i), src.at[0], w.at[i, z])
    for i, src in enumerate((gate_index, up_index, down_index)):
        copy_in(("k", i), src, keys.at[i])
    pl.semaphore_wait(barrier, len(ways))

    def landed(name, count):
        for i in range(count):
            local[name, i].wait()

    def piece(ref, hj, n, y_, x_):
        return ref.at[pl.ds(hj, n), y_, x_ // 2, half(x_)]

    def line_x(ref, hj, y_):
        return ref.at[hj, y_]

    def line_y(ref, hj, x_):
        return ref.at[hj, :, x_ // 2, half(x_)]

    def send_same(name, ref, way):
        cp.send(name, ref, ref, way)

    def gather_a(t, ref):
        for way in ("x+", "x-"):
            send_same((t, "a", way), piece(ref, 0, 2, y, x), way)
        for way in ("y+", "y-"):
            send_same((t, "a", way), piece(ref, 2, 2, y, x), way)

    def gather_b(t, ref, way):
        cp.recv((t, "a", way))
        hj, y_, x_ = {
            "x+": (0, y, xs[3]), "x-": (1, y, xs[1]), "y+": (2, ys[3], x), "y-": (3, ys[1], x),
        }[way]
        send_same((t, "b", way), piece(ref, hj, 1, y_, x_), way)

    def gather_c1(t, ref):
        cp.recv((t, "b", "x+"))
        cp.recv((t, "b", "x-"))
        for hj, way in ((0, "y+"), (1, "y-"), (1, "y+"), (0, "y-")):
            send_same((t, "c", way, hj), line_x(ref, hj, y), way)

    def gather_c2(t, ref):
        cp.recv((t, "b", "y+"))
        cp.recv((t, "b", "y-"))
        for hj, way in ((2, "x+"), (3, "x-"), (3, "x+"), (2, "x-")):
            send_same((t, "c", way, hj), line_y(ref, hj, x), way)

    def gather_d(t, ref, way):
        hj = {"y+": 0, "y-": 1, "x+": 2, "x-": 3}[way]
        cp.recv((t, "c", way, hj))
        part = {
            "y+": line_x(ref, 0, ys[3]), "y-": line_x(ref, 1, ys[1]),
            "x+": line_y(ref, 2, xs[3]), "x-": line_y(ref, 3, xs[1]),
        }[way]
        send_same((t, "d", way), part, way)

    def gather_end(t):
        for hj, way in ((1, "y+"), (0, "y-"), (3, "x+"), (2, "x-")):
            cp.recv((t, "c", way, hj))
        for way in ("y+", "y-", "x+", "x-"):
            cp.recv((t, "d", way))

    mine = core * 2

    def w_piece(i, o, first=0, n=2):
        return w.at[i, zs[o % 8], pl.ds(mine + first, n)]

    def weights_first(i):
        for way in ("z+", "z-"):
            send_same(("w", i, 1, way), w_piece(i, 0), way)

    def weights_step(i, k, way):
        o, first = (-k, 0) if way == "z+" else (k, 1)
        cp.recv(("w", i, k, way))
        if k < 3:
            send_same(("w", i, k + 1, way), w_piece(i, o), way)
        else:
            send_same(("w", i, 4, way), w_piece(i, o, first, 1), way)
        send_same(("ws", i, -o), w_piece(i, o), "c")

    def weights_far(i):
        cp.recv(("w", i, 4, "z+"))
        cp.recv(("w", i, 4, "z-"))
        send_same(("ws", i, 4), w_piece(i, 4), "c")

    def weights_end(i):
        for k in (1, 2, 3, 4, -1, -2, -3):
            cp.recv(("ws", i, k))

    line = (row * 2 + xl) * GROUP
    def picked(ref, first, p, axis=1):
        return jnp.concatenate(
            [block_of(ref, table[first + s, line + p]) for s in range(SLOTS)], axis=axis
        )

    def w_rows(i, p):
        return w[i, p].reshape(SLOTS * BLK, BLK)

    def w_lanes(i, p):
        return jnp.concatenate([w[i, p, s] for s in range(SLOTS)], axis=1)

    def forward(p, _):
        gate = dot(picked(xt, T_GATE, p), w_rows(0, p), ((1,), (0,)))
        up = dot(picked(xt, T_UP, p), w_rows(1, p), ((1,), (0,)))
        sig = jax.nn.sigmoid(gate)
        swish = gate * sig
        act = (swish * up).astype(BF16)
        act_s[p] = act
        swish_s[p] = swish
        slope_s[p] = up * (sig * (1.0 + gate * (1.0 - sig)))
        return 0

    def spread_out(p, _):
        spread = dot(act_s[p], w_lanes(2, p), ((1,), (0,)))
        for s in range(SLOTS):
            before = table[T_PREV_OUT + s, line + p]
            s_out[p * SLOTS + s] = s_out[before] + spread[:, s * BLK:(s + 1) * BLK]
        return 0

    def deltas(p, _):
        act_grad = dot(picked(xc, T_DOWN, p), w_lanes(2, p), ((1,), (1,)))
        gd_s[p] = (act_grad * slope_s[p]).astype(BF16)
        ud_s[p] = (act_grad * swish_s[p]).astype(BF16)
        return 0

    def backward(p, _):
        for i, delta, first in ((0, gd_s, T_PREV_GATE), (1, ud_s, T_PREV_UP)):
            back = dot(delta[p], w_rows(i, p), ((1,), (1,)))
            for s in range(SLOTS):
                before = table[first + s, line + p]
                s_in[p * 8 + i * SLOTS + s] = s_in[before] + back[:, s * BLK:(s + 1) * BLK]
        return 0

    def terms(j, _):
        odd = j % 2
        p = (z + 4 + (j // 2) * (1 - odd) - ((j + 1) // 2) * odd) % GROUP
        term = dot(act_s[p], picked(xc, T_DOWN, p), ((0,), (0,)))
        for s in range(SLOTS):
            grads[2, p, s] = term[:, s * BLK:(s + 1) * BLK].astype(BF16)
        for i, first, delta in ((0, T_GATE, gd_s), (1, T_UP, ud_s)):
            term = dot(picked(turned, first, p, axis=0), delta[p], ((1,), (0,)))
            grads[i, p] = term.astype(BF16).reshape(SLOTS, BLK, BLK)
        return 0

    def turn(q, _):
        turned[q // 8, (q // 2) % 4, q % 2] = xt[q // 8, (q // 2) % 4, q % 2].T
        return 0

    def panels(body, lower=0, upper=GROUP):
        lax.fori_loop(lower, upper, body, 0)

    def collect(dst, src, first):
        def body(q, _):
            dst[q // 8, (q // 2) % 4, q % 2] = src[table[first + q, 0]].astype(BF16)
            return 0

        lax.fori_loop(0, NBLK, body, 0)

    def stage(t, name, axis, hj, part, bufs, dims):
        near = xs if axis == "x" else ys
        plus, minus = axis + "+", axis + "-"
        b1, b2, b3 = bufs

        def first():
            cp.send((t, name, 1, plus), part(hj, near[2]), b1.at[0], plus)
            cp.send((t, name, 1, minus), part(hj + 1, near[2]), b1.at[1], minus)
            cp.send((t, name, 2, plus), part(hj + 1, near[1]), b2.at[0], plus)
            cp.send((t, name, 2, minus), part(hj, near[3]), b2.at[1], minus)

        def second(sign):
            way, part_, i = (
                (plus, part(hj, near[1]), 0) if sign == "+" else (minus, part(hj + 1, near[3]), 1)
            )
            cp.recv((t, name, 1, way))
            add_into(part_, [b1.at[i]], dims)
            cp.send((t, name, 3, way), part_, b3.at[i], way)

        def third():
            cp.recv((t, name, 2, plus))
            cp.recv((t, name, 2, minus))
            cp.recv((t, name, 3, plus))
            add_into(part(hj, near[0]), [b3.at[0], b2.at[1]], dims)
            cp.recv((t, name, 3, minus))
            add_into(part(hj + 1, near[0]), [b2.at[0], b3.at[1]], dims)

        return first, second, third

    def reduce_of(k, t, ref):
        def along_x(hj, y_):
            return ref.at[hj, y_]

        def along_y(hj, x_):
            return ref.at[hj, :, x_ // 2, half(x_)]

        def end_x(hj, x_):
            return ref.at[hj, y, x_ // 2, half(x_)]

        def end_y(hj, y_):
            return ref.at[hj, y_, xh, half(x)]

        y1 = stage(t, "y1", "y", 0, along_x, [ra.at[k, i] for i in range(3)], (2, 256, BLK))
        x1 = stage(t, "x1", "x", 2, along_y, [rb.at[k, i] for i in range(3)], (4, 128, BLK))
        x2 = stage(t, "x2", "x", 0, end_x, [qa.at[k, i] for i in range(3)], (128, BLK))
        y2 = stage(t, "y2", "y", 2, end_y, [qb.at[k, i] for i in range(3)], (128, BLK))
        return y1, x1, x2, y2

    o_y1, o_x1, o_x2, o_y2 = reduce_of(0, "o", b_out)
    i_y1, i_x1, i_x2, i_y2 = reduce_of(1, "i", b_in)

    theirs = (1 - core) * 2

    def sibling(o):
        p = zs[o % 8]
        cp.send(("gs", o), grads.at[:, p, pl.ds(theirs, 2)], g_sib.at[:, p], "c")

    def pair_sum(o):
        cp.recv(("gs", o))
        p = zs[o % 8]
        add_into(grads.at[:, p, pl.ds(mine, 2)], [g_sib.at[:, p]], (3, 2, 128, BLK))

    def z_send(way, k, s):
        d, sign, begins = (0, 1, 0) if way == "z+" else (1, -1, 1)
        part = grads.at[:, zs[sign * (5 - k) % 8], mine + s]
        if k > 2 or (k == 2 and s == begins):
            cp.recv(("z", way, k - 1, s))
            add_into(part, [rz.at[d, k - 2, s]], (3, 128, BLK))
        cp.send(("z", way, k, s), part, rz.at[d, k - 1, s], way)

    def z_last(s):
        cp.recv(("z", "z+", 4, s))
        cp.recv(("z", "z-", 4, s))

        def body(n, _):
            rows = pl.ds(pl.multiple_of((n % 2) * 64, 64), 64)
            i = n // 2
            grad_ref[i, mine + s, rows] = (
                grads[i, z, mine + s, rows].astype(F32)
                + rz[0, 3, s, i, rows].astype(F32)
                + rz[1, 3, s, i, rows].astype(F32)
            )
            return 0

        lax.fori_loop(0, 6, body, 0)
        part = grad_ref.at[:, mine + s]
        cp.send(("gf", s), part, part, "c")

    table_copy = pltpu.make_async_copy(tab, table, key_sem.at[0])

    def table_start():
        landed("k", 3)
        make_table(keys, tab, line)
        table_copy.start()

    def zeros():
        for ref in (xt, xc):
            ref[4, 0, 0] = jnp.zeros((256, BLK), BF16)
        turned[4, 0, 0] = jnp.zeros((BLK, 256), BF16)
        s_out[NBLK] = jnp.zeros((256, BLK), F32)
        s_in[2 * NBLK] = jnp.zeros((256, BLK), F32)

    def turn_some(lower, upper):
        lax.fori_loop(lower, upper, turn, 0)

    def write_out(ref, b):
        for hj in range(4):
            ref[:, hj * BLK:(hj + 1) * BLK] = b[hj, y, xh, half(x)]

    landed("t", 4)
    gather_a("t", xt)
    landed("w", 3)
    landed("c", 4)
    weights_first(0)
    weights_first(1)
    gather_a("c", xc)
    weights_first(2)
    table_start()
    table_copy.wait()
    zeros()
    gather_b("t", xt, "x+")
    gather_b("t", xt, "x-")
    gather_b("t", xt, "y+")
    gather_b("t", xt, "y-")
    weights_step(0, 1, "z+")
    weights_step(0, 1, "z-")
    gather_b("c", xc, "x+")
    gather_b("c", xc, "x-")
    gather_b("c", xc, "y+")
    weights_step(1, 1, "z+")
    weights_step(1, 1, "z-")
    gather_b("c", xc, "y-")
    weights_step(2, 1, "z+")
    weights_step(2, 1, "z-")
    gather_c1("t", xt)
    gather_c2("t", xt)
    weights_step(0, 2, "z+")
    weights_step(0, 2, "z-")
    weights_step(1, 2, "z+")
    weights_step(1, 2, "z-")
    weights_step(2, 2, "z+")
    weights_step(2, 2, "z-")
    gather_d("t", xt, "y+")
    gather_d("t", xt, "y-")
    weights_step(0, 3, "z+")
    gather_d("t", xt, "x+")
    gather_d("t", xt, "x-")
    weights_step(0, 3, "z-")
    gather_c1("c", xc)
    gather_c2("c", xc)
    weights_step(1, 3, "z+")
    weights_step(1, 3, "z-")
    weights_step(2, 3, "z+")
    weights_step(2, 3, "z-")
    weights_far(0)
    weights_end(0)
    weights_far(1)
    weights_end(1)
    gather_end("t")
    panels(forward, 0, 2)
    weights_far(2)
    panels(forward, 2, 4)
    weights_end(2)
    panels(spread_out, 0, 2)
    panels(spread_out, 2, 4)
    gather_d("c", xc, "x+")
    gather_d("c", xc, "x-")
    gather_d("c", xc, "y+")
    gather_d("c", xc, "y-")
    panels(forward, 4, 6)
    panels(spread_out, 4, 6)
    panels(forward, 6, 8)
    panels(spread_out, 6, 8)
    collect(b_out, s_out, T_LAST_OUT)
    o_y1[0]()
    o_x1[0]()
    turn_some(0, 16)
    turn_some(16, 32)
    gather_end("c")
    panels(deltas, 0, 2)
    panels(deltas, 2, 4)
    panels(deltas, 4, 6)
    panels(deltas, 6, 8)
    panels(terms, 0, 1)
    sibling(4)
    o_y1[1]("+")
    o_y1[1]("-")
    o_x1[1]("+")
    o_x1[1]("-")
    panels(backward, 0, 2)
    pair_sum(4)
    z_send("z+", 1, 0)
    z_send("z-", 1, 1)
    panels(backward, 2, 4)
    panels(backward, 4, 6)
    panels(backward, 6, 8)
    collect(b_in, s_in, T_LAST_IN)
    i_y1[0]()
    i_x1[0]()
    panels(terms, 1, 3)
    sibling(3)
    sibling(-3)
    o_y1[2]()
    o_x2[0]()
    o_x1[2]()
    pair_sum(3)
    z_send("z+", 2, 0)
    z_send("z+", 2, 1)
    pair_sum(-3)
    z_send("z-", 2, 1)
    z_send("z-", 2, 0)
    o_y2[0]()
    panels(terms, 3, 5)
    sibling(2)
    sibling(-2)
    i_y1[1]("+")
    i_y1[1]("-")
    i_x1[1]("+")
    i_x1[1]("-")
    panels(terms, 5, 7)
    sibling(1)
    sibling(-1)
    pair_sum(2)
    z_send("z+", 3, 0)
    pair_sum(-2)
    z_send("z-", 3, 1)
    o_x2[1]("+")
    o_x2[1]("-")
    pair_sum(1)
    o_y2[1]("+")
    pair_sum(-1)
    o_y2[1]("-")
    panels(terms, 7, 8)
    sibling(0)
    z_send("z+", 3, 1)
    z_send("z-", 3, 0)
    pair_sum(0)
    i_y1[2]()
    i_x2[0]()
    i_x1[2]()
    z_send("z+", 4, 0)
    i_y2[0]()
    z_send("z-", 4, 1)
    o_x2[2]()
    o_y2[2]()
    write_out(out_ref, b_out)
    z_send("z+", 4, 1)
    z_send("z-", 4, 0)
    i_x2[1]("+")
    i_x2[1]("-")
    i_y2[1]("+")
    i_y2[1]("-")
    i_x2[2]()
    i_y2[2]()
    write_out(in_ref, b_in)
    z_last(1)
    z_last(0)
    cp.recv(("gf", 1))
    cp.recv(("gf", 0))
    cp.finish()


def finish(out, in_grad, grads, out_, in_grad_, gate, up, down, sems):
    pairs = [(out, out_), (in_grad, in_grad_)]
    pairs += [(grads.at[i], ref.at[0]) for i, ref in enumerate((gate, up, down))]
    copies = [pltpu.make_async_copy(*pair, sems.at[i]) for i, pair in enumerate(pairs)]
    for copy in copies:
        copy.start()
    for copy in copies:
        copy.wait()


def per_device(
    tokens, cotangent, gate_blocks, up_blocks, down_blocks, gate_index, up_index, down_index
):
    hbm_spec = pl.BlockSpec(memory_space=pltpu.HBM)
    vmem_spec = pl.BlockSpec(memory_space=pltpu.VMEM)
    grad = jax.ShapeDtypeStruct((1, SLOTS, BLK, BLK), F32)
    act = jax.ShapeDtypeStruct((128, 4 * BLK), BF16)
    big = (4, 4, 2, 256, BLK)
    count = 190
    results = pl.pallas_call(
        kernel,
        out_shape=(act, act, jax.ShapeDtypeStruct((3, SLOTS, BLK, BLK), F32)),
        in_specs=[hbm_spec] * 8,
        out_specs=(vmem_spec,) * 3,
        scratch_shapes=[
            pltpu.VMEM((3, SLOTS, BLK), I32),
            pltpu.VMEM((T_ROWS, BLK), I32),
            pltpu.SMEM((T_ROWS, BLK), I32),
            pltpu.VMEM((5, 4, 2, 256, BLK), BF16),
            pltpu.VMEM((5, 4, 2, 256, BLK), BF16),
            pltpu.VMEM((5, 4, 2, BLK, 256), BF16),
            pltpu.VMEM((3, GROUP, SLOTS, BLK, BLK), BF16),
            pltpu.VMEM((NBLK + 1, 256, BLK), F32),
            pltpu.VMEM((2 * NBLK + 1, 256, BLK), F32),
            pltpu.VMEM((GROUP, 256, BLK), BF16),
            pltpu.VMEM((GROUP, 256, BLK), BF16),
            pltpu.VMEM((GROUP, 256, BLK), BF16),
            pltpu.VMEM((GROUP, 256, BLK), F32),
            pltpu.VMEM((GROUP, 256, BLK), F32),
            pltpu.VMEM(big, BF16),
            pltpu.VMEM(big, BF16),
            pltpu.VMEM((3, GROUP, SLOTS, BLK, BLK), BF16),
            pltpu.VMEM((2, 3, 2, 2, 256, BLK), BF16),
            pltpu.VMEM((2, 3, 2, 4, 128, BLK), BF16),
            pltpu.VMEM((2, 3, 2, 128, BLK), BF16),
            pltpu.VMEM((2, 3, 2, 128, BLK), BF16),
            pltpu.VMEM((3, GROUP, 2, BLK, BLK), BF16),
            pltpu.VMEM((2, 4, 2, 3, BLK, BLK), BF16),
            pltpu.SemaphoreType.DMA((1,)),
            pltpu.SemaphoreType.DMA((14,)),
            pltpu.SemaphoreType.DMA((count,)),
            pltpu.SemaphoreType.DMA((count,)),
        ],
        compiler_params=pltpu.CompilerParams(
            collective_id=0, has_side_effects=True, vmem_limit_bytes=60 << 20
        ),
        name="ffn",
    )(gate_index.T, up_index.T, down_index.T, tokens, cotangent, gate_blocks, up_blocks, down_blocks)
    return pl.pallas_call(
        finish,
        out_shape=(act, act, grad, grad, grad),
        in_specs=[vmem_spec] * 3,
        out_specs=(hbm_spec,) * 5,
        scratch_shapes=[pltpu.SemaphoreType.DMA((5,))],
        name="results",
    )(*results)


def solution(mesh):
    act = P(("dp", "col"), "row")
    blocks = P(("row", "col"), None, None, None)
    return jax.shard_map(
        per_device,
        mesh=mesh,
        in_specs=(act, act, blocks, blocks, blocks, P(), P(), P()),
        out_specs=(act, act, blocks, blocks, blocks),
        check_vma=False,
    )
```

time: 89.9 us -> 74.1 us (0.82)
  local copies, waits for them, and re-layouts: 8.24 us -> 0 us
  Pallas kernels: 79.9 us -> 73.4 us
    unnamed x19 -> x0, local copies, waits for them, and re-layouts: 6.94 us -> none
    pallas_call x1 -> x2, Pallas kernels: 79.9 us -> 73.4 us  [the longest x1 71.1 us: per_device(): pl.pallas_call(kernel, out_shape=(act, act, jax.ShapeDtypeStruct((3, SLOT...]
where the time goes in v2:
time: 74.1 us; the launch traced here: 74 us
  Pallas kernels  73.4 us (99%)
    pallas_call x1, Pallas kernels, per_device(): pl.pallas_call(kernel, out_shape=(act, act, jax.ShapeDtypeStruct((3, SLOT...  71.1 us
    pallas_call x1, Pallas kernels, per_device(): pl.pallas_call(finish, out_shape=(act, act, grad, grad, grad), in_specs=[...  2.28 us

profile of v2, /device:TPU:1, one launch (start us, length us, event | category | flops | bytes accessed | tf_op | source)
XLA Modules:
  0.0 74.0 jit_solution(5713241631929221512)
XLA Ops:
  0.6 71.1 %ffn.1 = (bf16[128,512]{1,0:T(8,128)(2,1)}, bf16[128,512]{1,0:T(8,128)(2,1)}, f32[3,4,128,128]{3,2,1,0:T(8,128)}) custom-call(s32[4,128]{1,0:T(4,128)} %bitcast.3, s32[4,128]{1,0:T(4,128)} %bitcast.4, s32[4,128]{1,0:T(4,128)} %bitcast.5, bf16[128,512]{1,0:T(8,128)(2,1)} %tokens.1, bf16[128,512]{1,0:T(8,128)(2,1)} %cotangent.1, ...), custom_call_target="tpu_custom_call" | custom-call | tf_op jit(solution)/shard_map/ffn/pallas_call | solution.py:611
  71.7 2.3 %results.1 = (bf16[128,512]{1,0:T(8,128)(2,1)}, bf16[128,512]{1,0:T(8,128)(2,1)}, f32[1,4,128,128]{3,2,1,0:T(8,128)}, f32[1,4,128,128]{3,2,1,0:T(8,128)}, f32[1,4,128,128]{3,2,1,0:T(8,128)}) custom-call(bf16[128,512]{1,0:T(8,128)(2,1)} %get-tuple-element.8.out, bf16[128,512]{1,0:T(8,128)(2,1)} %get-tuple-element.9.in_grad, ...), custom_call_target="tpu_custom_call" | custom-call | tf_op jit(solution)/shard_map/results/pallas_call | solution.py:650

commit v3 on v2

--- a/solution.py
+++ b/solution.py
@@ -9,6 +9,7 @@
 SLOTS = 4
 GROUP = 8
 NBLK = 32
+SENDS, RECVS = 40, 72
 F32 = jnp.float32
 BF16 = jnp.bfloat16
 MESH = pl.DeviceIdType.MESH
@@ -27,28 +28,52 @@
 
 
 class Copies:
-    def __init__(self, send_sem, recv_sem, neighbours):
-        self.send_sem, self.recv_sem, self.neighbours = send_sem, recv_sem, neighbours
-        self.made = {}
+    def __init__(self, send_sem, recv_sem, neighbours, back):
+        self.send_sem, self.recv_sem, self.neighbours, self.back = send_sem, recv_sem, neighbours, back
+        self.made, self.used, self.clock, self.recv_count = {}, [], 0, 0
+
+    def free(self, way):
+        heard = max(
+            (m["sent"] for m in self.made.values() if m["way"] == self.back.get(way, way) and m["got"]),
+            default=-1,
+        )
+        for m in self.made.values():
+            if m["way"] == way and m["held"] and m["got"] and m["got"] < heard:
+                m["held"] = False
+                return m["number"]
+        self.recv_count += 1
+        return self.recv_count - 1
 
     def send(self, name, src, dst, way):
-        number = len(self.made)
+        self.clock += 1
+        number = self.free(way)
+        if len(self.used) < SENDS:
+            slot = len(self.used)
+        else:
+            slot, earlier = self.used[-SENDS]
+            earlier.wait_send()
         copy = pltpu.make_async_remote_copy(
             src_ref=src,
             dst_ref=dst,
-            send_sem=self.send_sem.at[number],
+            send_sem=self.send_sem.at[slot],
             recv_sem=self.recv_sem.at[number],
             device_id=self.neighbours[way],
             device_id_type=MESH,
         )
         copy.start()
-        self.made[name] = copy
+        self.used.append((slot, copy))
+        self.made[name] = {
+            "copy": copy, "way": way, "number": number, "sent": self.clock, "got": 0, "held": True,
+        }
 
     def recv(self, name):
-        self.made[name].wait_recv()
+        self.clock += 1
+        self.made[name]["copy"].wait_recv()
+        self.made[name]["got"] = self.clock
 
     def finish(self):
-        for copy in self.made.values():
+        assert self.recv_count <= RECVS, self.recv_count
+        for _, copy in self.used[-SENDS:]:
             copy.wait_send()
 
 
@@ -150,11 +175,19 @@
         "x+": at(x=xs[1]), "x-": at(x=xs[3]), "y+": at(y=ys[1]), "y-": at(y=ys[3]),
         "z+": at(z=zs[1]), "z-": at(z=zs[7]), "c": at(core=1 - core),
     }
-    cp = Copies(send_sem, recv_sem, ways)
+    yp, yl = y // 2, y % 2
+    met = list(ways.values()) + [at(x=xs[2]), at(y=ys[2])]
+    ways.update({
+        ("x", 0): at(x=(1 - xh) * 2 + xl), ("x", 1): at(x=(1 - xh) * 2 + 1 - xl),
+        ("x", 2): at(x=xh * 2 + 1 - xl), ("y", 0): at(y=(1 - yp) * 2 + yl),
+        ("y", 1): at(y=(1 - yp) * 2 + 1 - yl), ("y", 2): at(y=yp * 2 + 1 - yl),
+    })
+    back = {"x+": "x-", "x-": "x+", "y+": "y-", "y-": "y+", "z+": "z-", "z-": "z+"}
+    cp = Copies(send_sem, recv_sem, ways, back)
 
     barrier = pltpu.get_barrier_semaphore()
-    for way in ways.values():
-        pl.semaphore_signal(barrier, inc=1, device_id=way, device_id_type=MESH)
+    for device in met:
+        pl.semaphore_signal(barrier, inc=1, device_id=device, device_id_type=MESH)
 
     def half(x_):
         return pl.ds(pl.multiple_of((x_ % 2) * 128, 128), 128)
@@ -173,7 +206,7 @@
         copy_in(("w", i), src.at[0], w.at[i, z])
     for i, src in enumerate((gate_index, up_index, down_index)):
         copy_in(("k", i), src, keys.at[i])
-    pl.semaphore_wait(barrier, len(ways))
+    pl.semaphore_wait(barrier, len(met))
 
     def landed(name, count):
         for i in range(count):
@@ -191,26 +224,30 @@
     def send_same(name, ref, way):
         cp.send(name, ref, ref, way)
 
-    def gather_a(t, ref):
-        for way in ("x+", "x-"):
-            send_same((t, "a", way), piece(ref, 0, 2, y, x), way)
-        for way in ("y+", "y-"):
-            send_same((t, "a", way), piece(ref, 2, 2, y, x), way)
+    def gather_a(t, ref, src):
+        for hj, way in ((0, "x+"), (1, "x-"), (2, "y+"), (3, "y-"), (1, "x+"), (0, "x-"), (3, "y+"), (2, "y-")):
+            cp.send(
+                (t, "a", way, hj), src.at[:, pl.ds(hj * BLK, BLK)], ref.at[hj, y, xh, half(x)], way
+            )
 
     def gather_b(t, ref, way):
-        cp.recv((t, "a", way))
         hj, y_, x_ = {
             "x+": (0, y, xs[3]), "x-": (1, y, xs[1]), "y+": (2, ys[3], x), "y-": (3, ys[1], x),
         }[way]
+        cp.recv((t, "a", way, hj))
         send_same((t, "b", way), piece(ref, hj, 1, y_, x_), way)
 
     def gather_c1(t, ref):
+        cp.recv((t, "a", "x+", 1))
+        cp.recv((t, "a", "x-", 0))
         cp.recv((t, "b", "x+"))
         cp.recv((t, "b", "x-"))
         for hj, way in ((0, "y+"), (1, "y-"), (1, "y+"), (0, "y-")):
             send_same((t, "c", way, hj), line_x(ref, hj, y), way)
 
     def gather_c2(t, ref):
+        cp.recv((t, "a", "y+", 3))
+        cp.recv((t, "a", "y-", 2))
         cp.recv((t, "b", "y+"))
         cp.recv((t, "b", "y-"))
         for hj, way in ((2, "x+"), (3, "x-"), (3, "x+"), (2, "x-")):
@@ -237,8 +274,9 @@
         return w.at[i, zs[o % 8], pl.ds(mine + first, n)]
 
     def weights_first(i):
+        src = (gate_blocks, up_blocks, down_blocks)[i].at[0, pl.ds(mine, 2)]
         for way in ("z+", "z-"):
-            send_same(("w", i, 1, way), w_piece(i, 0), way)
+            cp.send(("w", i, 1, way), src, w_piece(i, 0), way)
 
     def weights_step(i, k, way):
         o, first = (-k, 0) if way == "z+" else (k, 1)
@@ -254,9 +292,10 @@
         cp.recv(("w", i, 4, "z-"))
         send_same(("ws", i, 4), w_piece(i, 4), "c")
 
-    def weights_end(i):
-        for k in (1, 2, 3, 4, -1, -2, -3):
-            cp.recv(("ws", i, k))
+    def weights_end(i, k):
+        cp.recv(("ws", i, k))
+        if k < 4:
+            cp.recv(("ws", i, -k))
 
     line = (row * 2 + xl) * GROUP
     def picked(ref, first, p, axis=1):
@@ -270,7 +309,8 @@
     def w_lanes(i, p):
         return jnp.concatenate([w[i, p, s] for s in range(SLOTS)], axis=1)
 
-    def forward(p, _):
+    def forward(j, _):
+        p = (z + 8 + ((j + 1) // 2) * (2 * (j % 2) - 1)) % GROUP
         gate = dot(picked(xt, T_GATE, p), w_rows(0, p), ((1,), (0,)))
         up = dot(picked(xt, T_UP, p), w_rows(1, p), ((1,), (0,)))
         sig = jax.nn.sigmoid(gate)
@@ -282,10 +322,10 @@
         return 0
 
     def spread_out(p, _):
+        before = [s_out[table[T_PREV_OUT + s, line + p]] for s in range(SLOTS)]
         spread = dot(act_s[p], w_lanes(2, p), ((1,), (0,)))
         for s in range(SLOTS):
-            before = table[T_PREV_OUT + s, line + p]
-            s_out[p * SLOTS + s] = s_out[before] + spread[:, s * BLK:(s + 1) * BLK]
+            s_out[p * SLOTS + s] = before[s] + spread[:, s * BLK:(s + 1) * BLK]
         return 0
 
     def deltas(p, _):
@@ -296,10 +336,10 @@
 
     def backward(p, _):
         for i, delta, first in ((0, gd_s, T_PREV_GATE), (1, ud_s, T_PREV_UP)):
+            before = [s_in[table[first + s, line + p]] for s in range(SLOTS)]
             back = dot(delta[p], w_rows(i, p), ((1,), (1,)))
             for s in range(SLOTS):
-                before = table[first + s, line + p]
-                s_in[p * 8 + i * SLOTS + s] = s_in[before] + back[:, s * BLK:(s + 1) * BLK]
+                s_in[p * 8 + i * SLOTS + s] = before[s] + back[:, s * BLK:(s + 1) * BLK]
         return 0
 
     def terms(j, _):
@@ -327,34 +367,48 @@
 
         lax.fori_loop(0, NBLK, body, 0)
 
-    def stage(t, name, axis, hj, part, bufs, dims):
+    def stage(t, name, axis, hj, part, bufs, cut, dims, halves):
         near = xs if axis == "x" else ys
         plus, minus = axis + "+", axis + "-"
         b1, b2, b3 = bufs
 
         def first():
-            cp.send((t, name, 1, plus), part(hj, near[2]), b1.at[0], plus)
-            cp.send((t, name, 1, minus), part(hj + 1, near[2]), b1.at[1], minus)
-            cp.send((t, name, 2, plus), part(hj + 1, near[1]), b2.at[0], plus)
-            cp.send((t, name, 2, minus), part(hj, near[3]), b2.at[1], minus)
-
-        def second(sign):
-            way, part_, i = (
+            for n, far, mid in ((1, 2, (0, 1)), (2, 0, (1, 0))):
+                for h in range(halves):
+                    for d, way in enumerate((plus, minus)):
+                        there = near[2] if n == 1 else near[(1, 3)[d]]
+                        buf = (b1, b2)[n - 1].at[d]
+                        cp.send((t, name, n, way, h), cut(part(hj + mid[d], there), h), cut(buf, h), way)
+
+        def second(sign, h):
+            way, part_, d = (
                 (plus, part(hj, near[1]), 0) if sign == "+" else (minus, part(hj + 1, near[3]), 1)
             )
-            cp.recv((t, name, 1, way))
-            add_into(part_, [b1.at[i]], dims)
-            cp.send((t, name, 3, way), part_, b3.at[i], way)
-
-        def third():
-            cp.recv((t, name, 2, plus))
-            cp.recv((t, name, 2, minus))
-            cp.recv((t, name, 3, plus))
-            add_into(part(hj, near[0]), [b3.at[0], b2.at[1]], dims)
-            cp.recv((t, name, 3, minus))
-            add_into(part(hj + 1, near[0]), [b2.at[0], b3.at[1]], dims)
+            cp.recv((t, name, 1, way, h))
+            add_into(cut(part_, h), [cut(b1.at[d], h)], dims)
+            cp.send((t, name, 3, way, h), cut(part_, h), cut(b3.at[d], h), way)
+
+        def third(h):
+            cp.recv((t, name, 2, plus, h))
+            cp.recv((t, name, 2, minus, h))
+            cp.recv((t, name, 3, plus, h))
+            add_into(cut(part(hj, near[0]), h), [cut(b3.at[0], h), cut(b2.at[1], h)], dims)
+            cp.recv((t, name, 3, minus, h))
+            add_into(cut(part(hj + 1, near[0]), h), [cut(b2.at[0], h), cut(b3.at[1], h)], dims)
 
         return first, second, third
+
+    def direct(t, name, axis, part, buf):
+        def first(h):
+            for n in ((0, 1), (2,))[h]:
+                cp.send((t, name, n), part(n), buf.at[n], (axis, n))
+
+        def last():
+            for n in range(3):
+                cp.recv((t, name, n))
+            add_into(part(3), [buf.at[n] for n in range(3)], (2, 128, BLK))
+
+        return first, last
 
     def reduce_of(k, t, ref):
         def along_x(hj, y_):
@@ -363,16 +417,28 @@
         def along_y(hj, x_):
             return ref.at[hj, :, x_ // 2, half(x_)]
 
-        def end_x(hj, x_):
-            return ref.at[hj, y, x_ // 2, half(x_)]
-
-        def end_y(hj, y_):
-            return ref.at[hj, y_, xh, half(x)]
-
-        y1 = stage(t, "y1", "y", 0, along_x, [ra.at[k, i] for i in range(3)], (2, 256, BLK))
-        x1 = stage(t, "x1", "x", 2, along_y, [rb.at[k, i] for i in range(3)], (4, 128, BLK))
-        x2 = stage(t, "x2", "x", 0, end_x, [qa.at[k, i] for i in range(3)], (128, BLK))
-        y2 = stage(t, "y2", "y", 2, end_y, [qb.at[k, i] for i in range(3)], (128, BLK))
+        def end_x(n):
+            xh_, xl_ = (1 - xh if n < 2 else xh), (xl if n in (0, 3) else 1 - xl)
+            return ref.at[pl.ds(0, 2), y, xh_, half(xl_)]
+
+        def end_y(n):
+            yp_, yl_ = (1 - yp if n < 2 else yp), (yl if n in (0, 3) else 1 - yl)
+            return ref.at[pl.ds(2, 2), yp_ * 2 + yl_, xh, half(x)]
+
+        halves = 1 + k
+
+        def cut_x(part, h):
+            return part.at[xh if h else 1 - xh] if k else part
+
+        def cut_y(part, h):
+            return part.at[pl.ds((yp if h else 1 - yp) * 2, 2)] if k else part
+
+        dims = ((2, 256, BLK), (4, 128, BLK)) if k == 0 else ((256, BLK), (2, 128, BLK))
+
+        y1 = stage(t, "y1", "y", 0, along_x, [ra.at[k, i] for i in range(3)], cut_x, dims[0], halves)
+        x1 = stage(t, "x1", "x", 2, along_y, [rb.at[k, i] for i in range(3)], cut_y, dims[1], halves)
+        x2 = direct(t, "x2", "x", end_x, qa.at[k])
+        y2 = direct(t, "y2", "y", end_y, qb.at[k])
         return y1, x1, x2, y2
 
     o_y1, o_x1, o_x2, o_y2 = reduce_of(0, "o", b_out)
@@ -391,15 +457,17 @@
 
     def z_send(way, k, s):
         d, sign, begins = (0, 1, 0) if way == "z+" else (1, -1, 1)
-        part = grads.at[:, zs[sign * (5 - k) % 8], mine + s]
-        if k > 2 or (k == 2 and s == begins):
-            cp.recv(("z", way, k - 1, s))
-            add_into(part, [rz.at[d, k - 2, s]], (3, 128, BLK))
-        cp.send(("z", way, k, s), part, rz.at[d, k - 1, s], way)
+        for i, n in ((2, 1), (0, 2)):
+            part = grads.at[pl.ds(i, n), zs[sign * (5 - k) % 8], mine + s]
+            if k > 2 or (k == 2 and s == begins):
+                cp.recv(("z", way, k - 1, s, i))
+                add_into(part, [rz.at[d, k - 2, s, pl.ds(i, n)]], (n, 128, BLK))
+            cp.send(("z", way, k, s, i), part, rz.at[d, k - 1, s, pl.ds(i, n)], way)
 
     def z_last(s):
-        cp.recv(("z", "z+", 4, s))
-        cp.recv(("z", "z-", 4, s))
+        for i in (2, 0):
+            cp.recv(("z", "z+", 4, s, i))
+            cp.recv(("z", "z-", 4, s, i))
 
         def body(n, _):
             rows = pl.ds(pl.multiple_of((n % 2) * 64, 64), 64)
@@ -436,156 +504,168 @@
         for hj in range(4):
             ref[:, hj * BLK:(hj + 1) * BLK] = b[hj, y, xh, half(x)]
 
+    gather_a("t", xt, tokens)
+    weights_first(0)
+    weights_first(1)
+    gather_a("c", xc, cotangent)
+    weights_first(2)
+    table_start()
     landed("t", 4)
-    gather_a("t", xt)
     landed("w", 3)
     landed("c", 4)
-    weights_first(0)
-    weights_first(1)
-    gather_a("c", xc)
-    weights_first(2)
-    table_start()
     table_copy.wait()
     zeros()
     gather_b("t", xt, "x+")
     gather_b("t", xt, "x-")
     gather_b("t", xt, "y+")
     gather_b("t", xt, "y-")
-    weights_step(0, 1, "z+")
-    weights_step(0, 1, "z-")
     gather_b("c", xc, "x+")
     gather_b("c", xc, "x-")
     gather_b("c", xc, "y+")
+    gather_b("c", xc, "y-")
+    weights_step(0, 1, "z+")
+    weights_step(0, 1, "z-")
+    weights_end(0, 1)
+    gather_c1("t", xt)
+    gather_c2("t", xt)
     weights_step(1, 1, "z+")
     weights_step(1, 1, "z-")
-    gather_b("c", xc, "y-")
     weights_step(2, 1, "z+")
     weights_step(2, 1, "z-")
-    gather_c1("t", xt)
-    gather_c2("t", xt)
+    weights_end(1, 1)
+    weights_end(2, 1)
     weights_step(0, 2, "z+")
     weights_step(0, 2, "z-")
+    weights_end(0, 2)
     weights_step(1, 2, "z+")
     weights_step(1, 2, "z-")
+    gather_d("t", xt, "y+")
+    gather_d("t", xt, "y-")
+    gather_c1("c", xc)
+    gather_d("t", xt, "x+")
+    gather_d("t", xt, "x-")
+    gather_c2("c", xc)
+    weights_end(1, 2)
     weights_step(2, 2, "z+")
     weights_step(2, 2, "z-")
-    gather_d("t", xt, "y+")
-    gather_d("t", xt, "y-")
+    weights_end(2, 2)
     weights_step(0, 3, "z+")
-    gather_d("t", xt, "x+")
-    gather_d("t", xt, "x-")
     weights_step(0, 3, "z-")
-    gather_c1("c", xc)
-    gather_c2("c", xc)
+    weights_end(0, 3)
     weights_step(1, 3, "z+")
     weights_step(1, 3, "z-")
+    weights_end(1, 3)
     weights_step(2, 3, "z+")
+    gather_end("t")
     weights_step(2, 3, "z-")
+    panels(forward, 0, 1)
     weights_far(0)
-    weights_end(0)
+    panels(forward, 1, 3)
+    weights_end(2, 3)
+    panels(forward, 3, 5)
+    weights_end(0, 4)
     weights_far(1)
-    weights_end(1)
-    gather_end("t")
-    panels(forward, 0, 2)
-    weights_far(2)
-    panels(forward, 2, 4)
-    weights_end(2)
-    panels(spread_out, 0, 2)
-    panels(spread_out, 2, 4)
+    panels(forward, 5, 7)
     gather_d("c", xc, "x+")
     gather_d("c", xc, "x-")
     gather_d("c", xc, "y+")
     gather_d("c", xc, "y-")
-    panels(forward, 4, 6)
+    weights_end(1, 4)
+    panels(forward, 7, 8)
+    turn_some(0, 16)
+    weights_far(2)
+    turn_some(16, 32)
+    weights_end(2, 4)
+    panels(spread_out, 0, 2)
+    panels(spread_out, 2, 4)
     panels(spread_out, 4, 6)
-    panels(forward, 6, 8)
     panels(spread_out, 6, 8)
+    gather_end("c")
     collect(b_out, s_out, T_LAST_OUT)
     o_y1[0]()
     o_x1[0]()
-    turn_some(0, 16)
-    turn_some(16, 32)
-    gather_end("c")
     panels(deltas, 0, 2)
     panels(deltas, 2, 4)
     panels(deltas, 4, 6)
     panels(deltas, 6, 8)
     panels(terms, 0, 1)
     sibling(4)
-    o_y1[1]("+")
-    o_y1[1]("-")
-    o_x1[1]("+")
-    o_x1[1]("-")
+    panels(terms, 1, 3)
+    sibling(3)
+    sibling(-3)
     panels(backward, 0, 2)
     pair_sum(4)
     z_send("z+", 1, 0)
     z_send("z-", 1, 1)
+    pair_sum(3)
+    z_send("z+", 2, 1)
+    pair_sum(-3)
+    z_send("z-", 2, 0)
+    o_y1[1]("+", 0)
+    o_y1[1]("-", 0)
+    o_x1[1]("+", 0)
+    o_x1[1]("-", 0)
     panels(backward, 2, 4)
     panels(backward, 4, 6)
     panels(backward, 6, 8)
     collect(b_in, s_in, T_LAST_IN)
     i_y1[0]()
     i_x1[0]()
-    panels(terms, 1, 3)
-    sibling(3)
-    sibling(-3)
-    o_y1[2]()
-    o_x2[0]()
-    o_x1[2]()
-    pair_sum(3)
     z_send("z+", 2, 0)
-    z_send("z+", 2, 1)
-    pair_sum(-3)
     z_send("z-", 2, 1)
-    z_send("z-", 2, 0)
-    o_y2[0]()
     panels(terms, 3, 5)
     sibling(2)
     sibling(-2)
-    i_y1[1]("+")
-    i_y1[1]("-")
-    i_x1[1]("+")
-    i_x1[1]("-")
+    o_y1[2](0)
+    o_x2[0](0)
+    o_x2[0](1)
+    o_x1[2](0)
+    pair_sum(2)
+    z_send("z+", 3, 1)
+    pair_sum(-2)
+    z_send("z-", 3, 0)
+    i_y1[1]("+", 0)
+    i_y1[1]("-", 0)
+    i_x1[1]("+", 0)
+    i_x1[1]("-", 0)
+    i_y1[1]("+", 1)
+    i_y1[1]("-", 1)
+    o_y2[0](0)
+    i_x1[1]("+", 1)
+    i_x1[1]("-", 1)
+    z_send("z+", 3, 0)
+    z_send("z-", 3, 1)
+    o_y2[0](1)
     panels(terms, 5, 7)
     sibling(1)
     sibling(-1)
-    pair_sum(2)
-    z_send("z+", 3, 0)
-    pair_sum(-2)
-    z_send("z-", 3, 1)
-    o_x2[1]("+")
-    o_x2[1]("-")
-    pair_sum(1)
-    o_y2[1]("+")
-    pair_sum(-1)
-    o_y2[1]("-")
     panels(terms, 7, 8)
     sibling(0)
-    z_send("z+", 3, 1)
-    z_send("z-", 3, 0)
+    pair_sum(1)
+    z_send("z+", 4, 1)
+    pair_sum(-1)
+    z_send("z-", 4, 0)
     pair_sum(0)
-    i_y1[2]()
-    i_x2[0]()
-    i_x1[2]()
+    i_y1[2](0)
+    i_x2[0](0)
+    i_y1[2](1)
+    i_x2[0](1)
     z_send("z+", 4, 0)
-    i_y2[0]()
     z_send("z-", 4, 1)
-    o_x2[2]()
-    o_y2[2]()
+    o_x2[1]()
+    i_x1[2](0)
+    i_y2[0](0)
+    o_y2[1]()
     write_out(out_ref, b_out)
-    z_send("z+", 4, 1)
-    z_send("z-", 4, 0)
-    i_x2[1]("+")
-    i_x2[1]("-")
-    i_y2[1]("+")
-    i_y2[1]("-")
-    i_x2[2]()
-    i_y2[2]()
+    i_x1[2](1)
+    i_y2[0](1)
+    z_last(0)
+    z_last(1)
+    i_x2[1]()
+    i_y2[1]()
     write_out(in_ref, b_in)
-    z_last(1)
-    z_last(0)
+    cp.recv(("gf", 0))
     cp.recv(("gf", 1))
-    cp.recv(("gf", 0))
     cp.finish()
 
 
@@ -607,7 +687,6 @@
     grad = jax.ShapeDtypeStruct((1, SLOTS, BLK, BLK), F32)
     act = jax.ShapeDtypeStruct((128, 4 * BLK), BF16)
     big = (4, 4, 2, 256, BLK)
-    count = 190
     results = pl.pallas_call(
         kernel,
         out_shape=(act, act, jax.ShapeDtypeStruct((3, SLOTS, BLK, BLK), F32)),
@@ -639,8 +718,8 @@
             pltpu.VMEM((2, 4, 2, 3, BLK, BLK), BF16),
             pltpu.SemaphoreType.DMA((1,)),
             pltpu.SemaphoreType.DMA((14,)),
-            pltpu.SemaphoreType.DMA((count,)),
-            pltpu.SemaphoreType.DMA((count,)),
+            pltpu.SemaphoreType.DMA((SENDS,)),
+            pltpu.SemaphoreType.DMA((RECVS,)),
         ],
         compiler_params=pltpu.CompilerParams(
             collective_id=0, has_side_effects=True, vmem_limit_bytes=60 << 20

time: 74.1 us -> 70.1 us (0.946)
  Pallas kernels: 73.4 us -> 69.3 us
    pallas_call x1, Pallas kernels: 71.1 us -> 67.1 us  [per_device(): pl.pallas_call(kernel, out_shape=(act, act, jax.ShapeDtypeStruct((3, SLOT...]
where the time goes in v3:
time: 70.1 us; the launch traced here: 70 us
  Pallas kernels  69.3 us (99%)
    pallas_call x1, Pallas kernels, per_device(): pl.pallas_call(kernel, out_shape=(act, act, jax.ShapeDtypeStruct((3, SLOT...  67.1 us
    pallas_call x1, Pallas kernels, per_device(): pl.pallas_call(finish, out_shape=(act, act, grad, grad, grad), in_specs=[...  2.28 us

profile of v3, /device:TPU:1, one launch (start us, length us, event | category | flops | bytes accessed | tf_op | source)
XLA Modules:
  0.0 70.0 jit_solution(14277869965173771480)
XLA Ops:
  0.6 67.1 %ffn.1 = (bf16[128,512]{1,0:T(8,128)(2,1)}, bf16[128,512]{1,0:T(8,128)(2,1)}, f32[3,4,128,128]{3,2,1,0:T(8,128)}) custom-call(s32[4,128]{1,0:T(4,128)} %bitcast.3, s32[4,128]{1,0:T(4,128)} %bitcast.4, s32[4,128]{1,0:T(4,128)} %bitcast.5, bf16[128,512]{1,0:T(8,128)(2,1)} %tokens.1, bf16[128,512]{1,0:T(8,128)(2,1)} %cotangent.1, ...), custom_call_target="tpu_custom_call" | custom-call | tf_op jit(solution)/shard_map/ffn/pallas_call | solution.py:690
  67.7 2.3 %results.1 = (bf16[128,512]{1,0:T(8,128)(2,1)}, bf16[128,512]{1,0:T(8,128)(2,1)}, f32[1,4,128,128]{3,2,1,0:T(8,128)}, f32[1,4,128,128]{3,2,1,0:T(8,128)}, f32[1,4,128,128]{3,2,1,0:T(8,128)}) custom-call(bf16[128,512]{1,0:T(8,128)(2,1)} %get-tuple-element.8.out, bf16[128,512]{1,0:T(8,128)(2,1)} %get-tuple-element.9.in_grad, ...), custom_call_target="tpu_custom_call" | custom-call | tf_op jit(solution)/shard_map/results/pallas_call | solution.py:729

commit v4 on v3

--- a/solution.py
+++ b/solution.py
@@ -9,7 +9,7 @@
 SLOTS = 4
 GROUP = 8
 NBLK = 32
-SENDS, RECVS = 40, 72
+SENDS, RECVS = 40, 77
 F32 = jnp.float32
 BF16 = jnp.bfloat16
 MESH = pl.DeviceIdType.MESH
@@ -96,7 +96,7 @@
         dst[index] = value.astype(dst.dtype)
         return 0
 
-    lax.fori_loop(0, total * per, body, 0)
+    lax.fori_loop(0, total * per, body, 0, unroll=2)
 
 
 def make_table(keys, tab, first):
@@ -358,14 +358,14 @@
         return 0
 
     def panels(body, lower=0, upper=GROUP):
-        lax.fori_loop(lower, upper, body, 0)
+        lax.fori_loop(lower, upper, body, 0, unroll=upper - lower)
 
     def collect(dst, src, first):
         def body(q, _):
             dst[q // 8, (q // 2) % 4, q % 2] = src[table[first + q, 0]].astype(BF16)
             return 0
 
-        lax.fori_loop(0, NBLK, body, 0)
+        lax.fori_loop(0, NBLK, body, 0, unroll=4)
 
     def stage(t, name, axis, hj, part, bufs, cut, dims, halves):
         near = xs if axis == "x" else ys
@@ -498,7 +498,7 @@
         s_in[2 * NBLK] = jnp.zeros((256, BLK), F32)
 
     def turn_some(lower, upper):
-        lax.fori_loop(lower, upper, turn, 0)
+        lax.fori_loop(lower, upper, turn, 0, unroll=4)
 
     def write_out(ref, b):
         for hj in range(4):
@@ -526,28 +526,28 @@
     weights_step(0, 1, "z+")
     weights_step(0, 1, "z-")
     weights_end(0, 1)
+    weights_step(1, 1, "z+")
+    weights_step(1, 1, "z-")
     gather_c1("t", xt)
     gather_c2("t", xt)
-    weights_step(1, 1, "z+")
-    weights_step(1, 1, "z-")
+    weights_end(1, 1)
     weights_step(2, 1, "z+")
     weights_step(2, 1, "z-")
-    weights_end(1, 1)
     weights_end(2, 1)
     weights_step(0, 2, "z+")
     weights_step(0, 2, "z-")
     weights_end(0, 2)
     weights_step(1, 2, "z+")
     weights_step(1, 2, "z-")
+    weights_end(1, 2)
     gather_d("t", xt, "y+")
     gather_d("t", xt, "y-")
-    gather_c1("c", xc)
+    weights_step(2, 2, "z+")
+    weights_step(2, 2, "z-")
     gather_d("t", xt, "x+")
     gather_d("t", xt, "x-")
+    gather_c1("c", xc)
     gather_c2("c", xc)
-    weights_end(1, 2)
-    weights_step(2, 2, "z+")
-    weights_step(2, 2, "z-")
     weights_end(2, 2)
     weights_step(0, 3, "z+")
     weights_step(0, 3, "z-")
@@ -556,34 +556,34 @@
     weights_step(1, 3, "z-")
     weights_end(1, 3)
     weights_step(2, 3, "z+")
+    weights_step(2, 3, "z-")
     gather_end("t")
-    weights_step(2, 3, "z-")
+    weights_end(2, 3)
     panels(forward, 0, 1)
     weights_far(0)
     panels(forward, 1, 3)
-    weights_end(2, 3)
     panels(forward, 3, 5)
+    weights_far(1)
     weights_end(0, 4)
-    weights_far(1)
     panels(forward, 5, 7)
     gather_d("c", xc, "x+")
     gather_d("c", xc, "x-")
     gather_d("c", xc, "y+")
+    weights_end(1, 4)
     gather_d("c", xc, "y-")
-    weights_end(1, 4)
     panels(forward, 7, 8)
+    weights_far(2)
     turn_some(0, 16)
-    weights_far(2)
-    turn_some(16, 32)
     weights_end(2, 4)
     panels(spread_out, 0, 2)
     panels(spread_out, 2, 4)
     panels(spread_out, 4, 6)
     panels(spread_out, 6, 8)
-    gather_end("c")
     collect(b_out, s_out, T_LAST_OUT)
     o_y1[0]()
     o_x1[0]()
+    turn_some(16, 32)
+    gather_end("c")
     panels(deltas, 0, 2)
     panels(deltas, 2, 4)
     panels(deltas, 4, 6)
@@ -611,59 +611,59 @@
     collect(b_in, s_in, T_LAST_IN)
     i_y1[0]()
     i_x1[0]()
-    z_send("z+", 2, 0)
-    z_send("z-", 2, 1)
     panels(terms, 3, 5)
     sibling(2)
     sibling(-2)
-    o_y1[2](0)
-    o_x2[0](0)
-    o_x2[0](1)
-    o_x1[2](0)
+    z_send("z+", 2, 0)
+    z_send("z-", 2, 1)
+    panels(terms, 5, 7)
+    sibling(1)
+    sibling(-1)
     pair_sum(2)
     z_send("z+", 3, 1)
     pair_sum(-2)
     z_send("z-", 3, 0)
     i_y1[1]("+", 0)
+    pair_sum(1)
+    pair_sum(-1)
     i_y1[1]("-", 0)
     i_x1[1]("+", 0)
     i_x1[1]("-", 0)
+    o_y1[2](0)
     i_y1[1]("+", 1)
     i_y1[1]("-", 1)
-    o_y2[0](0)
     i_x1[1]("+", 1)
     i_x1[1]("-", 1)
+    o_x2[0](0)
+    o_x2[0](1)
+    o_x1[2](0)
+    o_y2[0](0)
+    o_y2[0](1)
     z_send("z+", 3, 0)
     z_send("z-", 3, 1)
-    o_y2[0](1)
-    panels(terms, 5, 7)
-    sibling(1)
-    sibling(-1)
     panels(terms, 7, 8)
     sibling(0)
-    pair_sum(1)
     z_send("z+", 4, 1)
-    pair_sum(-1)
     z_send("z-", 4, 0)
     pair_sum(0)
     i_y1[2](0)
     i_x2[0](0)
+    i_x1[2](0)
+    i_y2[0](0)
     i_y1[2](1)
     i_x2[0](1)
+    i_x1[2](1)
+    i_y2[0](1)
     z_send("z+", 4, 0)
     z_send("z-", 4, 1)
+    o_y2[1]()
     o_x2[1]()
-    i_x1[2](0)
-    i_y2[0](0)
-    o_y2[1]()
     write_out(out_ref, b_out)
-    i_x1[2](1)
-    i_y2[0](1)
+    i_y2[1]()
+    i_x2[1]()
+    write_out(in_ref, b_in)
     z_last(0)
     z_last(1)
-    i_x2[1]()
-    i_y2[1]()
-    write_out(in_ref, b_in)
     cp.recv(("gf", 0))
     cp.recv(("gf", 1))
     cp.finish()

time: 70.1 us -> 67.1 us (0.957)
  Pallas kernels: 69.3 us -> 66.3 us
    pallas_call x1, Pallas kernels: 67.1 us -> 64 us  [per_device(): pl.pallas_call(kernel, out_shape=(act, act, jax.ShapeDtypeStruct((3, SLOT...]
where the time goes in v4:
time: 67.1 us; the launch traced here: 66.9 us
  Pallas kernels  66.3 us (99%)
    pallas_call x1, Pallas kernels, per_device(): pl.pallas_call(kernel, out_shape=(act, act, jax.ShapeDtypeStruct((3, SLOT...  64 us
    pallas_call x1, Pallas kernels, per_device(): pl.pallas_call(finish, out_shape=(act, act, grad, grad, grad), in_specs=[...  2.28 us

profile of v4, /device:TPU:1, one launch (start us, length us, event | category | flops | bytes accessed | tf_op | source)
XLA Modules:
  0.0 66.9 jit_solution(4936442113603890886)
XLA Ops:
  0.6 64.0 %ffn.1 = (bf16[128,512]{1,0:T(8,128)(2,1)}, bf16[128,512]{1,0:T(8,128)(2,1)}, f32[3,4,128,128]{3,2,1,0:T(8,128)}) custom-call(s32[4,128]{1,0:T(4,128)} %bitcast.3, s32[4,128]{1,0:T(4,128)} %bitcast.4, s32[4,128]{1,0:T(4,128)} %bitcast.5, bf16[128,512]{1,0:T(8,128)(2,1)} %tokens.1, bf16[128,512]{1,0:T(8,128)(2,1)} %cotangent.1, ...), custom_call_target="tpu_custom_call" | custom-call | tf_op jit(solution)/shard_map/ffn/pallas_call | solution.py:690
  64.7 2.3 %results.1 = (bf16[128,512]{1,0:T(8,128)(2,1)}, bf16[128,512]{1,0:T(8,128)(2,1)}, f32[1,4,128,128]{3,2,1,0:T(8,128)}, f32[1,4,128,128]{3,2,1,0:T(8,128)}, f32[1,4,128,128]{3,2,1,0:T(8,128)}) custom-call(bf16[128,512]{1,0:T(8,128)(2,1)} %get-tuple-element.8.out, bf16[128,512]{1,0:T(8,128)(2,1)} %get-tuple-element.9.in_grad, ...), custom_call_target="tpu_custom_call" | custom-call | tf_op jit(solution)/shard_map/results/pallas_call | solution.py:729

commit v5 on v4

--- a/solution.py
+++ b/solution.py
@@ -154,10 +154,11 @@
 
 def kernel(
     gate_index, up_index, down_index, tokens, cotangent, gate_blocks, up_blocks, down_blocks,
+    out_hbm, in_hbm, grad_hbm,
     out_ref, in_ref, grad_ref,
     keys, tab, table, xt, xc, turned, w, s_out, s_in, act_s, gd_s, ud_s, swish_s, slope_s,
     b_out, b_in, grads, ra, rb, qa, qb, g_sib, rz,
-    key_sem, local_sem, send_sem, recv_sem,
+    key_sem, local_sem, out_sem, send_sem, recv_sem,
 ):
     core = lax.axis_index("dp")
     row = lax.axis_index("row")
@@ -500,9 +501,15 @@
     def turn_some(lower, upper):
         lax.fori_loop(lower, upper, turn, 0, unroll=4)
 
+    out_copy, in_copy, grad_copy = (
+        pltpu.make_async_copy(src, dst, out_sem.at[n])
+        for n, (src, dst) in enumerate(((out_ref, out_hbm), (in_ref, in_hbm), (grad_ref, grad_hbm)))
+    )
+
     def write_out(ref, b):
         for hj in range(4):
             ref[:, hj * BLK:(hj + 1) * BLK] = b[hj, y, xh, half(x)]
+        (out_copy if ref is out_ref else in_copy).start()
 
     gather_a("t", xt, tokens)
     weights_first(0)
@@ -666,7 +673,10 @@
     z_last(1)
     cp.recv(("gf", 0))
     cp.recv(("gf", 1))
+    grad_copy.start()
     cp.finish()
+    for copy in (out_copy, in_copy, grad_copy):
+        copy.wait()
 
 
 def finish(out, in_grad, grads, out_, in_grad_, gate, up, down, sems):
@@ -691,8 +701,11 @@
         kernel,
         out_shape=(act, act, jax.ShapeDtypeStruct((3, SLOTS, BLK, BLK), F32)),
         in_specs=[hbm_spec] * 8,
-        out_specs=(vmem_spec,) * 3,
+        out_specs=(hbm_spec,) * 3,
         scratch_shapes=[
+            pltpu.VMEM((128, 4 * BLK), BF16),
+            pltpu.VMEM((128, 4 * BLK), BF16),
+            pltpu.VMEM((3, SLOTS, BLK, BLK), F32),
             pltpu.VMEM((3, SLOTS, BLK), I32),
             pltpu.VMEM((T_ROWS, BLK), I32),
             pltpu.SMEM((T_ROWS, BLK), I32),
@@ -718,6 +731,7 @@
             pltpu.VMEM((2, 4, 2, 3, BLK, BLK), BF16),
             pltpu.SemaphoreType.DMA((1,)),
             pltpu.SemaphoreType.DMA((14,)),
+            pltpu.SemaphoreType.DMA((3,)),
             pltpu.SemaphoreType.DMA((SENDS,)),
             pltpu.SemaphoreType.DMA((RECVS,)),
         ],

time: 67.1 us -> 66.8 us (level)
  no operation moved by 1% of the time
where the time goes in v5:
time: 66.8 us; the launch traced here: 66.7 us
  Pallas kernels  66.1 us (99%)
    pallas_call x1, Pallas kernels, per_device(): pl.pallas_call(kernel, out_shape=(act, act, jax.ShapeDtypeStruct((3, SLOT...  63.8 us
    pallas_call x1, Pallas kernels, per_device(): pl.pallas_call(finish, out_shape=(act, act, grad, grad, grad), in_specs=[...  2.28 us

profile of v5, /device:TPU:1, one launch (start us, length us, event | category | flops | bytes accessed | tf_op | source)
XLA Modules:
  0.0 66.7 jit_solution(15082064853308061071)
XLA Ops:
  0.6 63.8 %ffn.1 = (bf16[128,512]{1,0:T(8,128)(2,1)}, bf16[128,512]{1,0:T(8,128)(2,1)}, f32[3,4,128,128]{3,2,1,0:T(8,128)}) custom-call(s32[4,128]{1,0:T(4,128)} %bitcast.3, s32[4,128]{1,0:T(4,128)} %bitcast.4, s32[4,128]{1,0:T(4,128)} %bitcast.5, bf16[128,512]{1,0:T(8,128)(2,1)} %tokens.1, bf16[128,512]{1,0:T(8,128)(2,1)} %cotangent.1, ...), custom_call_target="tpu_custom_call" | custom-call | tf_op jit(solution)/shard_map/ffn/pallas_call | solution.py:700
  64.4 2.3 %results.1 = (bf16[128,512]{1,0:T(8,128)(2,1)}, bf16[128,512]{1,0:T(8,128)(2,1)}, f32[1,4,128,128]{3,2,1,0:T(8,128)}, f32[1,4,128,128]{3,2,1,0:T(8,128)}, f32[1,4,128,128]{3,2,1,0:T(8,128)}) custom-call(bf16[128,512]{1,0:T(8,128)(2,1)} %get-tuple-element.8.out, bf16[128,512]{1,0:T(8,128)(2,1)} %get-tuple-element.9.in_grad, ...), custom_call_target="tpu_custom_call" | custom-call | tf_op jit(solution)/shard_map/results/pallas_call | solution.py:743
